TPU v7x, 256 devices: a whole 4x4x8 slice. The times are simulated.
256 devices in a mesh: row: 4 (over y), space: 64 (over z, x, core).
Axes of the slice: x: 4, y: 4, z: 8, core: 2. Of those that a mesh axis runs over, the one named last changes fastest.
Arguments:
- right_side: float32 [4, 9, 5, 32768], P('row', None, None, 'space'), may hold values from -6 to 6
- coupling: float32 [4, 6, 5, 32768], P('row', None, None, 'space'), may hold values from -0.5 to 0.5
- offsets: int32 [4, 6, 32768], P('row', None, 'space'), may hold values from -16 to 16
- block_mean: float32 [4, 5, 5, 32768], P('row', None, None, 'space'), may hold values from -0.179 to 1.51, as said below
- block_wave: float32 [4, 4, 10, 10, 32768], P('row', None, None, None, 'space'), may hold values from -0.127 to 1.51, as said below
- donor_cells: int32 [4, 1024], P('row'), may hold values from 0 to 32767
- receiver_cells: int32 [4, 1024], P('row'), may hold values from 0 to 32767
- inlet_gain: float32 [4, 5, 1024], P('row'), may hold values from 0.5 to 2
Outputs:
- solution: float32 [4, 9, 5, 32768], P('row', None, None, 'space')
Inputs may be any that keep to these rules, and one draw needn't show every extreme that they name: `block_mean`: each block has a diagonal in 0.5 .. 1.5 and smaller entries off it. `block_wave`: each block has a diagonal in 0.5 .. 1.5 and smaller entries off it.
All inputs are finite; a program needn't handle non-finite values.
Results may differ from a plain program's by a relative error of at most 0.0001.
Values sent between devices are 32-bit elements; how exact they have to be, the bound alone decides.
A program may use at most 128 MiB of HBM per device.

v0:
```python
import math

import jax
import jax.numpy as jnp
from jax import lax
from jax.sharding import PartitionSpec as P

NI = 9
NV = 5
HALO = 16
SWEEPS = 2
NIF = 1024


def with_halo(block, sides, width):
    for axis, dim in sides:
        count = lax.axis_size(axis)
        forward = [(i, i + 1) for i in range(count - 1)]
        backward = [(target, source) for source, target in forward]
        low = lax.ppermute(
            lax.slice_in_dim(block, block.shape[dim] - width, None, axis=dim), axis, forward
        )
        high = lax.ppermute(lax.slice_in_dim(block, 0, width, axis=dim), axis, backward)
        block = jnp.concatenate([low, block, high], axis=dim)
    return block


def from_behind(value, axis, steps):
    count = lax.axis_size(axis)
    first, last = (max(0, -steps), min(count, count - steps))
    return lax.ppermute(value, axis, [(source, source + steps) for source in range(first, last)])


def spectral_table(instances):
    position = jnp.arange(instances).astype(jnp.float32)
    harmonic = jnp.arange(1, (instances - 1) // 2 + 1).astype(jnp.float32)
    phase_angle = 2.0 * math.pi / instances * harmonic[:, None] * position[None, :]
    weight = math.sqrt(2.0 / instances)
    wave_rows = jnp.stack(
        [weight * jnp.cos(phase_angle), weight * jnp.sin(phase_angle)], axis=1
    ).reshape(-1, instances)
    mean_row = jnp.full((1, instances), 1.0 / math.sqrt(instances), jnp.float32)
    return jnp.concatenate([mean_row, wave_rows], axis=0)


def invert_blocks(values, block_mean, block_wave, spectral):
    spectral_modes = jnp.einsum("kn,nvc->kvc", spectral, values, precision=lax.Precision.HIGHEST)
    variables = spectral_modes.shape[1]
    harmonics = (spectral_modes.shape[0] - 1) // 2
    steady = jnp.sum(block_mean * spectral_modes[0][None, :, :], axis=1)
    paired = spectral_modes[1:].reshape(harmonics, 2 * variables, spectral_modes.shape[2])
    paired = jnp.sum(block_wave * paired[:, None, :, :], axis=2)
    joined = jnp.concatenate(
        [steady[None], paired.reshape(2 * harmonics, variables, spectral_modes.shape[2])], axis=0
    )
    return jnp.einsum("kn,kvc->nvc", spectral, joined, precision=lax.Precision.HIGHEST)


def neighbor_sum(padded, offsets, coupling, reach_cells):
    cell_count = offsets.shape[1]
    cell_base = jnp.arange(cell_count, dtype=jnp.int32) + reach_cells
    accumulated = jnp.zeros((padded.shape[0], padded.shape[1], cell_count), jnp.float32)
    for neighbor in range(offsets.shape[0]):
        neighbor_vals = jnp.take(padded, cell_base + offsets[neighbor], axis=2)
        accumulated = accumulated + coupling[neighbor][None, :, :] * neighbor_vals
    return accumulated


def on_device(
    right_side, coupling, offsets, block_mean, block_wave, donor_cells, receiver_cells, inlet_gain
):
    space_rank = lax.axis_index("space")
    source_base = right_side[0]
    cell_count = source_base.shape[2]
    spectral = spectral_table(source_base.shape[0])
    first_cell = space_rank * cell_count
    mean_blocks = block_mean[0]
    wave_blocks = block_wave[0]

    def apply_inverse(values):
        return invert_blocks(values, mean_blocks, wave_blocks, spectral)

    donor_local = donor_cells[0] - first_cell
    donor_inside = ((donor_local >= 0) & (donor_local < cell_count)).astype(jnp.float32)
    donor_clip = jnp.clip(donor_local, 0, cell_count - 1)
    receiver_local = receiver_cells[0] - first_cell
    receiver_inside = ((receiver_local >= 0) & (receiver_local < cell_count)).astype(jnp.float32)
    receiver_clip = jnp.clip(receiver_local, 0, cell_count - 1)
    row_total = lax.axis_size("row")
    inlet_profile = jnp.zeros((NI, NV, NIF), jnp.float32)
    state_field = source_base
    for row_step in range(row_total):
        inflow = inlet_gain[0][None, :, :] * inlet_profile * receiver_inside[None, None, :]
        source = source_base - jnp.zeros_like(source_base).at[:, :, receiver_clip].add(inflow)
        state_field = apply_inverse(source)
        for sweep_index in range(SWEEPS):
            padded = with_halo(state_field, (("space", 2),), HALO)
            coupled = neighbor_sum(padded, offsets[0], coupling[0], HALO)
            state_field = apply_inverse(source - coupled)
        if row_step + 1 < row_total:
            outgoing = jnp.take(state_field, donor_clip, axis=2) * donor_inside[None, None, :]
            summed = lax.psum(outgoing, "space")
            arrived = from_behind(summed, "row", 1)
            inlet_profile = arrived
    return state_field[None]


def solution(mesh):
    return jax.shard_map(
        on_device,
        mesh=mesh,
        in_specs=(
            P("row", None, None, "space"),
            P("row", None, None, "space"),
            P("row", None, "space"),
            P("row", None, None, "space"),
            P("row", None, None, None, "space"),
            P("row", None),
            P("row", None),
            P("row", None, None),
        ),
        out_specs=P("row", None, None, "space"),
        check_vma=False,
    )
```

profile of v0, /device:TPU:25, one launch (start us, length us, event | category | flops | bytes accessed | tf_op | source)
XLA Modules:
  0.0 1396.9 jit_solution(15716528840691371441)
XLA Ops:
  11.8 75.5 %scatter_fusion = f32[9,5,512]{0,1,2:T(8,128)S(1)} fusion(f32[9,5,512]{0,1,2:T(8,128)S(1)} %broadcast.193.clone.2, s32[1024]{0:T(1024)S(1)} %bitcast.521, f32[1024,9,5]{1,2,0:T(8,128)} %copy.291), kind=kCustom, calls=%fused_computation.51 | custom fusion | flops 46080 | bytes 557056 | tf_op jit(solution)/shard_map/scatter-add | solution.py:94
  89.4 3.6 collective-permute-start
  100.9 2.7 gather_fusion
  103.6 2.9 copy.300
  109.3 2.9 copy.302
  112.1 2.7 gather_fusion.2
  114.9 2.9 copy.304
  117.8 2.7 gather_fusion.3
  120.5 2.9 copy.306
  123.4 2.7 gather_fusion.4
  126.1 2.9 copy.308
  161.6 3.0 copy.318
  164.6 2.9 copy.320
  168.9 3.0 copy.324
  171.9 2.9 copy.326
  181.1 9.1 gather_fusion.12
  190.2 9.4 bitcast_multiply_fusion.2
  199.7 200.8 %all-reduce.5.cloned.1.call-done = f32[9,5,1024]{0,1,2:T(8,128)} async-done(((f32[9,5,1024]{0,1,2:T(8,128)}), f32[9,5,1024]{0,1,2:T(8,128)}) %all-reduce.5.cloned.1.call-update) | async-done | bytes 184336 | tf_op jit(solution)/shard_map/psum | solution.py:102
  400.5 2.9 copy.336
  404.9 6.6 collective-permute-done.4
  414.4 75.5 %scatter_fusion.1 = f32[9,5,512]{0,1,2:T(8,128)S(1)} fusion(f32[9,5,512]{0,1,2:T(8,128)S(1)} %broadcast.193.clone.1, s32[1024]{0:T(1024)S(1)} %bitcast.522, f32[1024,9,5]{1,2,0:T(8,128)} %copy.337), kind=kCustom, calls=%fused_computation.52 | custom fusion | flops 46080 | bytes 557056 | tf_op jit(solution)/shard_map/scatter-add | solution.py:94
  493.5 5.9 collective-permute-start.5
  501.4 3.4 collective-permute-done.6
  523.6 3.0 copy.346
  526.6 2.9 copy.348
  530.9 3.0 copy.352
  533.9 2.9 copy.354
  542.8 2.9 collective-permute-start.8
  566.9 3.0 copy.364
  569.9 2.9 copy.366
  574.2 3.0 copy.370
  577.2 2.9 copy.372
  586.4 9.1 gather_fusion.25
  595.5 9.4 bitcast_multiply_fusion.1
  605.0 198.8 %all-reduce.7.cloned.1.call-done = f32[9,5,1024]{0,1,2:T(8,128)} async-done(((f32[9,5,1024]{0,1,2:T(8,128)}), f32[9,5,1024]{0,1,2:T(8,128)}) %all-reduce.7.cloned.1.call-update) | async-done | bytes 184336 | tf_op jit(solution)/shard_map/psum | solution.py:102
  803.8 2.9 copy.382
  808.2 6.6 collective-permute-done.9
  817.7 75.5 %scatter_fusion.2 = f32[9,5,512]{0,1,2:T(8,128)S(1)} fusion(f32[9,5,512]{0,1,2:T(8,128)S(1)} %broadcast.193.clone, s32[1024]{0:T(1024)S(1)} %bitcast.523, f32[1024,9,5]{1,2,0:T(8,128)} %copy.383), kind=kCustom, calls=%fused_computation.53 | custom fusion | flops 46080 | bytes 557056 | tf_op jit(solution)/shard_map/scatter-add | solution.py:94
  896.8 5.9 collective-permute-start.10
  904.7 3.4 collective-permute-done.11
  926.8 3.0 copy.392
  929.9 2.9 copy.394
  934.2 3.0 copy.398
  937.2 2.9 copy.400
  946.0 2.8 collective-permute-start.13
  970.2 3.0 copy.410
  973.2 2.9 copy.412
  977.5 3.0 copy.416
  980.5 2.9 copy.418
  989.7 9.1 gather_fusion.38
  998.8 9.4 bitcast_multiply_fusion
  1008.2 199.0 %all-reduce.9.cloned.1.call-done = f32[9,5,1024]{0,1,2:T(8,128)} async-done(((f32[9,5,1024]{0,1,2:T(8,128)}), f32[9,5,1024]{0,1,2:T(8,128)}) %all-reduce.9.cloned.1.call-update) | async-done | bytes 184336 | tf_op jit(solution)/shard_map/psum | solution.py:102
  1207.2 2.9 copy.428
  1211.5 6.7 collective-permute-done.14
  1221.1 75.5 %scatter_fusion.3 = f32[9,5,512]{0,1,2:T(8,128)S(1)} fusion(f32[9,5,512]{0,1,2:T(8,128)S(1)} %broadcast.193, s32[1024]{0:T(1024)S(1)} %bitcast.524, f32[1024,9,5]{1,2,0:T(8,128)} %copy.429), kind=kCustom, calls=%fused_computation.54 | custom fusion | flops 46080 | bytes 557056 | tf_op jit(solution)/shard_map/scatter-add | solution.py:94
  1300.2 5.9 collective-permute-start.15
  1308.1 3.4 collective-permute-done.16
  1330.2 3.0 copy.438
  1333.3 2.9 copy.440
  1337.6 3.0 copy.444
  1340.6 2.9 copy.446
  1373.5 3.0 copy.456
  1378.0 3.0 copy.460
  1382.4 3.0 copy.464
  (402 shorter events, 254.5 us)
Async XLA Ops:
  6.5 394.0 %all-reduce.5.cloned.1.call-start = ((), (), s32[]{:S(2)}) async-start(), calls=%async_computation | async-start | bytes 8388608 | tf_op jit(solution)/shard_map/psum | solution.py:102
  11.6 76.4 %copy-start.17 = (f32[1,9,5,512]{3,0,2,1:T(1,128)S(1)}, f32[1,9,5,512]{3,0,2,1:T(1,128)}, u32[]{:S(2)}) copy-start(f32[1,9,5,512]{3,0,2,1:T(1,128)} %param.12) | copy-start | bytes 276484
  11.8 76.9 %copy-start = (f32[1,4,10,10,512]{4,1,3,2,0:T(4,128)S(1)}, f32[1,4,10,10,512]{4,1,3,2,0:T(4,128)}, u32[]{:S(2)}) copy-start(f32[1,4,10,10,512]{4,1,3,2,0:T(4,128)} %param.16) | copy-start | bytes 2457604
  87.3 1.6 copy-start.1
  88.0 7.4 copy-start.26
  88.1 7.5 copy-start.25
  88.1 7.6 copy-start.24
  89.4 6.4 collective-permute-start
  93.0 5.3 collective-permute-start.1
  131.7 2.3 copy-start.18
  131.7 2.3 copy-start.19
  131.7 2.3 copy-start.20
  131.7 2.3 copy-start.21
  131.7 2.3 copy-start.22
  135.5 4.5 collective-permute-start.2
  137.4 5.3 collective-permute-start.3
  161.6 5.9 copy-start.11
  168.9 5.9 copy-start.5
  199.6 205.3 %copy-start.23 = (f32[1,5,1024]{2,0,1:T(1,128)S(1)}, f32[1,5,1024]{2,0,1:T(1,128)}, u32[]{:S(2)}) copy-start(f32[1,5,1024]{2,0,1:T(1,128)} %param.19) | copy-start | bytes 61444
  199.6 604.2 %all-reduce.7.cloned.1.call-start = ((), (), s32[]{:S(2)}) async-start(), calls=%async_computation.1 | async-start | bytes 8388608 | tf_op jit(solution)/shard_map/psum | solution.py:102
  403.4 8.1 collective-permute-start.4
  493.5 7.8 collective-permute-start.5
  499.4 5.3 collective-permute-start.6
  523.6 5.9 copy-start.12
  530.9 5.9 copy-start.6
  540.8 4.8 collective-permute-start.7
  542.8 5.3 collective-permute-start.8
  566.9 5.9 copy-start.13
  574.2 5.9 copy-start.7
  604.9 602.3 %all-reduce.9.cloned.1.call-start = ((), (), s32[]{:S(2)}) async-start(), calls=%async_computation.2 | async-start | bytes 8388608 | tf_op jit(solution)/shard_map/psum | solution.py:102
  806.7 8.1 collective-permute-start.9
  896.8 7.8 collective-permute-start.10
  902.7 5.3 collective-permute-start.11
  926.8 5.9 copy-start.14
  934.2 5.9 copy-start.8
  944.1 4.7 collective-permute-start.12
  946.0 5.3 collective-permute-start.13
  970.2 5.9 copy-start.15
  977.5 5.9 copy-start.9
  1210.1 8.1 collective-permute-start.14
  1300.2 7.8 collective-permute-start.15
  1306.1 5.3 collective-permute-start.16
  1330.2 5.9 copy-start.16
  1337.5 5.9 copy-start.10
  1347.5 4.5 collective-permute-start.17
  1349.4 5.3 collective-permute-start.18
  1373.5 3.0 copy-start.2
  1378.0 3.0 copy-start.3
  1382.4 3.0 copy-start.4
Sparse Core Ops, SparseCore 0:
  199.7 200.7 all-reduce.4
  605.1 198.6 all-reduce.6
  1008.3 198.8 all-reduce.8
where the time goes:
time: 1420 us; the launch traced here: 1400 us
  waiting for transfers between devices  642 us (45%)
  other arithmetic  354 us (25%)
  local copies, waits for them, and re-layouts  324 us (23%)
  starting transfers between devices  52.5 us (4%)
  between operations  15.4 us (1%)
    psum x3, waiting for transfers between devices, on_device(): summed = lax.psum(outgoing, 'space')  599 us
    scatter-add x4, other arithmetic, on_device(): jnp.zeros_like(source_base).at[:, :, receiver_clip].add(inflow)  302 us
    gather x96, local copies, waits for them, and re-layouts, neighbor_sum(): neighbor_vals = jnp.take(padded, cell_base + offsets[neighbor], axis=2)  248 us
    ppermute x8, starting transfers between devices, with_halo(): lax.ppermute(lax.slice_in_dim(block, block.shape[dim] - width, None, axis...  28.9 us
  transfers between devices with their start and end apart: 22, of which 14 were waited for; matrix products, arithmetic and copies ran while one was open for 0% of the time, Pallas kernels for 0%

commit v1 on v0

--- a/solution.py
+++ b/solution.py
@@ -1,15 +1,473 @@
+import functools
 import math
 
 import jax
 import jax.numpy as jnp
+import numpy as np
 from jax import lax
+from jax.experimental import pallas as pl
+from jax.experimental.pallas import tpu as pltpu
 from jax.sharding import PartitionSpec as P
 
 NI = 9
 NV = 5
+NF = NI * NV
+NOFF = 6
 HALO = 16
 SWEEPS = 2
 NIF = 1024
+ROWS = 4
+NS = 64
+OWN = 512
+EDGE = 32
+CAP = 8
+MESH = pl.DeviceIdType.MESH
+
+HALO_ROWS = 152
+AT_SIX = 144
+AT_FIVE = 104
+AT_TAIL = 80
+
+
+def spectral_numbers():
+    n = np.arange(NI, dtype=np.float64)
+    table = [np.full(NI, 1.0 / math.sqrt(NI))]
+    for k in range(1, (NI - 1) // 2 + 1):
+        table.append(math.sqrt(2.0 / NI) * np.cos(2.0 * math.pi * k * n / NI))
+        table.append(math.sqrt(2.0 / NI) * np.sin(2.0 * math.pi * k * n / NI))
+    return np.stack(table).astype(np.float32)
+
+
+def kernel(
+    rhs_h, cpl_h, off_h, bm_h, bw_h, don_h, rec_h, gain_h,
+    out_ref, flag_ref,
+    rhs_v, cpl_v, off_v, bm_v, bw_v, gain_v, idx_v,
+    wave_w, five_w, six_w, lane_w, src_w, x_w, y_w,
+    send_left, send_right, from_left, from_right,
+    code_s, sel_s, xr_s, wr_s, gpk_s, msg_s, got_s,
+    in_sem, idx_send, idx_recv, edge_send, edge_recv, msg_send, msg_recv,
+):
+    r = lax.axis_index("row")
+    s = lax.axis_index("space")
+
+    loads = [
+        pltpu.make_async_copy(bw_h.at[0], bw_v, in_sem.at[0]),
+        pltpu.make_async_copy(bm_h.at[0], bm_v, in_sem.at[1]),
+        pltpu.make_async_copy(cpl_h.at[0], cpl_v, in_sem.at[2]),
+        pltpu.make_async_copy(rhs_h.at[0], rhs_v, in_sem.at[3]),
+        pltpu.make_async_copy(off_h.at[0], off_v, in_sem.at[4]),
+        pltpu.make_async_copy(gain_h.at[0], gain_v, in_sem.at[5]),
+        pltpu.make_async_copy(don_h, idx_v.at[r, 0], in_sem.at[6]),
+        pltpu.make_async_copy(rec_h, idx_v.at[r, 1], in_sem.at[7]),
+    ]
+    for c in loads:
+        c.start()
+
+    bar = pltpu.get_barrier_semaphore()
+
+    def greet(row, t):
+        pl.semaphore_signal(bar, inc=1, device_id=(row, t), device_id_type=MESH)
+
+    @pl.when(s > 0)
+    def _():
+        greet(r, s - 1)
+
+    @pl.when(s < NS - 1)
+    def _():
+        greet(r, s + 1)
+
+    for row in range(ROWS):
+        @pl.when((row > r + 1) | (row < r - 1))
+        def _():
+            greet(row, s)
+
+    @pl.when(r < ROWS - 1)
+    def _():
+        def one(t, c):
+            greet(r + 1, t)
+            return c
+        lax.fori_loop(0, NS, one, 0, unroll=8)
+
+    @pl.when(r > 0)
+    def _():
+        def one(t, c):
+            greet(r - 1, t)
+            return c
+        lax.fori_loop(0, NS, one, 0, unroll=8)
+
+    lane8 = lax.broadcasted_iota(jnp.int32, (8, 128), 1)
+
+    def to_windows(tiles, dst, row):
+        n = tiles[0].shape[0]
+        lane = lane8[:n]
+        up = [pltpu.roll(t, 32, 1) for t in tiles]
+        down = [pltpu.roll(t, 96, 1) for t in tiles]
+        for m in range(4):
+            even = up[m] if m == 0 else jnp.where(lane < 32, up[m - 1], up[m])
+            odd = down[m] if m == 3 else jnp.where(lane < 96, down[m], down[m + 1])
+            dst[pl.ds(row + 2 * m, n, stride=8), :] = even
+            dst[pl.ds(row + 2 * m + 1, n, stride=8), :] = odd
+
+    def pack(firsts, lasts, row):
+        n = firsts[0].shape[0]
+        lane = lane8[:n]
+        left = firsts[0]
+        right = pltpu.roll(lasts[0], 32, 1)
+        for e in range(1, len(firsts)):
+            left = jnp.where(lane >= 32 * e, pltpu.roll(firsts[e], 32 * e, 1), left)
+            moved = lasts[e] if e == 3 else pltpu.roll(lasts[e], (32 * e + 32) % 128, 1)
+            right = jnp.where(lane >= 32 * e, moved, right)
+        send_left[pl.ds(row, n), :] = left
+        send_right[pl.ds(row, n), :] = right
+
+    def read_tiles(ref, lead, rows):
+        return [ref[(*lead, pl.ds(rows[0], rows[1]), pl.ds(128 * m, 128))] for m in range(4)]
+
+    loads[0].wait()
+
+    def wave_rows(f, c):
+        for g0, n, row in ((0, 8, f * 8), (8, 2, AT_TAIL + f * 2)):
+            firsts, lasts = [], []
+            for k in range(4):
+                tiles = read_tiles(bw_v, (k, f), (g0, n))
+                to_windows(tiles, wave_w, ((k * 10 + f) * 10 + g0) * 8)
+                firsts.append(tiles[0])
+                lasts.append(tiles[3])
+            pack(firsts, lasts, row)
+        return c
+
+    lax.fori_loop(0, 10, wave_rows, 0)
+
+    for c in loads[1:5]:
+        c.wait()
+    fives = [(bm_v, i) for i in range(5)] + [(cpl_v, j) for j in range(6)] + [(rhs_v, n) for n in range(9)]
+    for p in range(5):
+        firsts, lasts = [], []
+        for e in range(4):
+            ref, i = fives[4 * p + e]
+            tiles = read_tiles(ref, (i,), (0, 5))
+            to_windows(tiles, five_w, (4 * p + e) * 40)
+            firsts.append(tiles[0])
+            lasts.append(tiles[3])
+        pack(firsts, lasts, AT_FIVE + 8 * p)
+    tiles = [off_v[:, pl.ds(128 * m, 128)].astype(jnp.float32) for m in range(4)]
+    to_windows(tiles, six_w, 0)
+    pack([tiles[0]], [tiles[3]], AT_SIX)
+    send_left[pl.ds(100, 4), :] = jnp.zeros((4, 128), jnp.float32)
+    send_right[pl.ds(100, 4), :] = jnp.zeros((4, 128), jnp.float32)
+    for p in range(5):
+        send_left[pl.ds(AT_FIVE + 8 * p + 5, 3), :] = jnp.zeros((3, 128), jnp.float32)
+        send_right[pl.ds(AT_FIVE + 8 * p + 5, 3), :] = jnp.zeros((3, 128), jnp.float32)
+    send_left[pl.ds(AT_SIX + 6, 2), :] = jnp.zeros((2, 128), jnp.float32)
+    send_right[pl.ds(AT_SIX + 6, 2), :] = jnp.zeros((2, 128), jnp.float32)
+    for c in loads[5:]:
+        c.wait()
+    xr_s[...] = jnp.zeros(xr_s.shape, jnp.bfloat16)
+    src_w[pl.ds(NF * 8, 24), :] = jnp.zeros((24, 128), jnp.float32)
+    x_w[pl.ds(NF * 8, 24), :] = jnp.zeros((24, 128), jnp.float32)
+
+    @pl.when(s == 0)
+    def _():
+        from_left[...] = jnp.zeros(from_left.shape, jnp.float32)
+
+    @pl.when(s == NS - 1)
+    def _():
+        from_right[...] = jnp.zeros(from_right.shape, jnp.float32)
+
+    def one_if(condition):
+        return jnp.where(condition, 1, 0)
+
+    here = one_if(s > 0) + one_if(s < NS - 1)
+    here = here + (NS - 1) * (one_if(r > 0) + one_if(r < ROWS - 1)) + ROWS - 1
+    pl.semaphore_wait(bar, here)
+
+    right = pltpu.make_async_remote_copy(
+        send_right, from_left, edge_send.at[0], edge_recv.at[0],
+        device_id=(r, lax.rem(s + 1, NS)), device_id_type=MESH)
+    left = pltpu.make_async_remote_copy(
+        send_left, from_right, edge_send.at[1], edge_recv.at[1],
+        device_id=(r, lax.rem(s + NS - 1, NS)), device_id_type=MESH)
+
+    @pl.when(s < NS - 1)
+    def _():
+        right.start()
+
+    @pl.when(s > 0)
+    def _():
+        left.start()
+
+    index_copies = [
+        pltpu.make_async_remote_copy(
+            idx_v.at[r], idx_v.at[r], idx_send.at[d], idx_recv.at[d],
+            device_id=(lax.rem(r + d, ROWS), s), device_id_type=MESH)
+        for d in range(1, ROWS)
+    ]
+    for c in index_copies:
+        c.start()
+    for c in index_copies:
+        c.wait()
+
+    dev64 = lax.broadcasted_iota(jnp.int32, (NS, 1), 0)
+    tri = (lax.broadcasted_iota(jnp.int32, (128, 128), 0) <= lax.broadcasted_iota(jnp.int32, (128, 128), 1))
+    tri = tri.astype(jnp.float32).astype(jnp.bfloat16)
+
+    def order(mask):
+        before = jnp.zeros((NS, 1), jnp.float32)
+        for b in range(NIF // 128):
+            m = mask[:, 128 * b:128 * b + 128]
+            upto = jnp.dot(m.astype(jnp.bfloat16), tri, preferred_element_type=jnp.float32)
+            code_s[:, pl.ds(128 * b, 128)] = jnp.where(m > 0.5, before + upto - 1.0, -1.0)
+            before = before + jnp.sum(m, axis=1, keepdims=True)
+
+    def pick(k, value):
+        return jnp.sum(jnp.where(code_s[...] == float(k), value, 0.0), axis=1, keepdims=True)
+
+    def in_block(cells, device):
+        low = device * OWN
+        return (cells >= low) & (cells < low + OWN)
+
+    def in_windows(cells, device):
+        low = device * OWN - EDGE
+        return (cells >= low) & (cells < low + OWN + 2 * EDGE)
+
+    @pl.when(r < ROWS - 1)
+    def _():
+        donor = idx_v[r, 0]
+        receiver = idx_v[r + 1, 1]
+        order((in_block(donor, s) & in_windows(receiver, dev64)).astype(jnp.float32))
+        place = (donor - s * OWN + 1).astype(jnp.float32)
+        cell = lax.broadcasted_iota(jnp.int32, (NS, OWN), 1).astype(jnp.float32) + 1.0
+        for k in range(CAP):
+            hit = (pick(k, place) == cell).astype(jnp.float32).astype(jnp.bfloat16)
+            sel_s[pl.ds((k % 4) * NS, NS), pl.ds((k // 4) * OWN, OWN)] = hit
+
+    @pl.when(r > 0)
+    def _():
+        donor = idx_v[r - 1, 0]
+        receiver = idx_v[r, 1]
+        order((in_block(donor, dev64) & in_windows(receiver, s)).astype(jnp.float32))
+        place = (receiver - s * OWN + EDGE + 1).astype(jnp.float32)
+        position = lax.broadcasted_iota(jnp.int32, (NS, 1024), 1)
+        cell = ((position // 128) * 64 + position % 128 + 1).astype(jnp.float32)
+        lane = lax.broadcasted_iota(jnp.int32, (1, 128), 1)
+        field = lane % 64
+        for k in range(CAP):
+            hit = (pick(k, place) == cell).astype(jnp.float32).astype(jnp.bfloat16)
+            wr_s[pl.ds(k * NS, NS), :] = hit
+        for k in range(4):
+            rows = jnp.zeros((NS, 128), jnp.float32)
+            for v in range(NV):
+                gain = gain_v[pl.ds(v, 1), :]
+                mine = (field % NV == v) & (field < NF)
+                rows = rows + jnp.where(mine & (lane < 64), pick(k, gain), 0.0)
+                rows = rows + jnp.where(mine & (lane >= 64), pick(k + 4, gain), 0.0)
+            gpk_s[pl.ds(k * NS, NS), :] = rows
+
+    @pl.when(s > 0)
+    def _():
+        right.wait_recv()
+
+    @pl.when(s < NS - 1)
+    def _():
+        left.wait_recv()
+
+    def merge(dst, row, n, src_row, e):
+        lane = lane8[:n]
+        low = from_left[pl.ds(src_row, n), :]
+        low = low if e == 0 else pltpu.roll(low, 128 - 32 * e, 1)
+        high = from_right[pl.ds(src_row, n), :]
+        high = high if e == 3 else pltpu.roll(high, 96 - 32 * e, 1)
+        at = pl.ds(row, n, stride=8)
+        dst[at, :] = jnp.where(lane < 32, low, dst[at, :])
+        at = pl.ds(row + 7, n, stride=8)
+        dst[at, :] = jnp.where(lane >= 96, high, dst[at, :])
+
+    def wave_edges(f, c):
+        for k in range(4):
+            merge(wave_w, (k * 10 + f) * 80, 8, f * 8, k)
+            merge(wave_w, (k * 10 + f) * 80 + 64, 2, AT_TAIL + f * 2, k)
+        return c
+
+    lax.fori_loop(0, 10, wave_edges, 0)
+    for p in range(5):
+        for e in range(4):
+            merge(five_w, (4 * p + e) * 40, 5, AT_FIVE + 8 * p, e)
+    merge(six_w, 0, 6, AT_SIX, 0)
+
+    for j in range(NOFF):
+        at = lane8 + six_w[pl.ds(8 * j, 8), :].astype(jnp.int32)
+        lane_w[j] = jnp.clip(at, 0, 127)
+
+    table = spectral_numbers()
+    for v in range(NV):
+        parts = [five_w[pl.ds((55 + n * NV + v) * 8, 8), :] for n in range(NI)]
+        for m in range(NI):
+            total = float(table[m, 0]) * parts[0]
+            for n in range(1, NI):
+                total = total + float(table[m, n]) * parts[n]
+            src_w[pl.ds((m * NV + v) * 8, 8), :] = total
+
+    @pl.when(r > 0)
+    def _():
+        pltpu.make_async_remote_copy(
+            msg_s, got_s, msg_send, msg_recv, device_id=(r - 1, s), device_id_type=MESH).wait_recv()
+        rows = jnp.concatenate([got_s[:, k, :] for k in range(4)], axis=0) * gpk_s[...]
+        turned = jnp.concatenate([rows[:128].T, rows[128:].T], axis=1)
+        both = jnp.concatenate([turned[:48], turned[64:112]], axis=1)
+        high = both.astype(jnp.bfloat16)
+        low = (both - high.astype(jnp.float32)).astype(jnp.bfloat16)
+        inflow = jnp.dot(jnp.concatenate([high, low], axis=0), wr_s[...], preferred_element_type=jnp.float32)
+        inflow = inflow[:48] + inflow[48:]
+        for a in range(6):
+            for j in range(8):
+                at = pl.ds(a * 64 + j, 8, stride=8)
+                src_w[at, :] = src_w[at, :] - inflow[8 * a:8 * a + 8, 128 * j:128 * j + 128]
+
+    def relax(first, count, block, stride):
+        source = [src_w[pl.ds((first + f) * 8, 8), :] for f in range(count)]
+
+        def solve(values):
+            result = []
+            for f in range(count):
+                total = None
+                for g in range(count):
+                    term = block[pl.ds(stride + (f * count + g) * 8, 8), :] * values[g]
+                    total = term if total is None else total + term
+                result.append(total)
+            return result
+
+        x = solve(source)
+        for _ in range(SWEEPS):
+            rest = []
+            for f in range(count):
+                total = source[f]
+                for j in range(NOFF):
+                    moved = jnp.take_along_axis(x[f], lane_w[j], axis=1, mode="promise_in_bounds")
+                    total = total - five_w[pl.ds((25 + j * NV + f % NV) * 8, 8), :] * moved
+                rest.append(total)
+            x = solve(rest)
+        for f in range(count):
+            x_w[pl.ds((first + f) * 8, 8), :] = x[f]
+
+    relax(0, NV, five_w, 0)
+
+    def harmonic(k, c):
+        relax(NV + 10 * k, 10, wave_w, k * 800)
+        return c
+
+    lax.fori_loop(0, 4, harmonic, 0)
+
+    def own_tile(ref, row, n, m):
+        lane = lane8[:n]
+        even = ref[pl.ds(row + 2 * m, n, stride=8), :]
+        odd = ref[pl.ds(row + 2 * m + 1, n, stride=8), :]
+        return jnp.where(lane < 64, pltpu.roll(even, 96, 1), pltpu.roll(odd, 32, 1))
+
+    @pl.when(r < ROWS - 1)
+    def _():
+        for a in range(3):
+            for m in range(4):
+                tile = jnp.concatenate([own_tile(x_w, (2 * a + i) * 64, 8, m) for i in range(2)], axis=0)
+                high = tile.astype(jnp.bfloat16)
+                low = (tile - high.astype(jnp.float32)).astype(jnp.bfloat16)
+                for half in range(2):
+                    at = pl.ds(half * OWN + 128 * m, 128)
+                    xr_s[pl.ds(64 * half + 16 * a, 16), at] = high
+                    xr_s[pl.ds(128 + 64 * half + 16 * a, 16), at] = low
+        values = lax.dot_general(
+            sel_s[...], xr_s[...], (((1,), (1,)), ((), ())), preferred_element_type=jnp.float32)
+        values = values[:, :128] + values[:, 128:]
+        for k in range(4):
+            msg_s[:, k, :] = values[k * NS:(k + 1) * NS]
+
+        def send(j, c):
+            t = lax.rem(s + j, NS)
+            pltpu.make_async_remote_copy(
+                msg_s.at[t], got_s.at[s], msg_send, msg_recv,
+                device_id=(r + 1, t), device_id_type=MESH).start()
+            return c
+
+        lax.fori_loop(0, NS, send, 0, unroll=8)
+
+    for v in range(NV):
+        parts = [x_w[pl.ds((m * NV + v) * 8, 8), :] for m in range(NI)]
+        for n in range(NI):
+            total = float(table[0, n]) * parts[0]
+            for m in range(1, NI):
+                total = total + float(table[m, n]) * parts[m]
+            y_w[pl.ds((n * NV + v) * 8, 8), :] = total
+    for n in range(NI):
+        for m in range(4):
+            out_ref[0, n, :, pl.ds(128 * m, 128)] = own_tile(y_w, n * 40, 5, m)
+
+    most = jnp.zeros((NS, NS), jnp.float32)
+    for row in range(ROWS - 1):
+        gives = in_block(idx_v[row, 0], dev64).astype(jnp.float32).astype(jnp.bfloat16)
+        takes = in_windows(idx_v[row + 1, 1], dev64).astype(jnp.float32).astype(jnp.bfloat16)
+        count = lax.dot_general(gives, takes, (((1,), (1,)), ((), ())), preferred_element_type=jnp.float32)
+        most = jnp.maximum(most, count)
+    flag_ref[...] = jnp.broadcast_to((jnp.max(most, keepdims=True) > CAP + 0.5).astype(jnp.int32), (8, 128))
+
+    @pl.when(s < NS - 1)
+    def _():
+        right.wait_send()
+
+    @pl.when(s > 0)
+    def _():
+        left.wait_send()
+
+    @pl.when(r < ROWS - 1)
+    def _():
+        pltpu.make_async_remote_copy(
+            msg_s, got_s, msg_send, msg_recv, device_id=(r + 1, s), device_id_type=MESH).wait_send()
+
+
+def fast(*args):
+    any_space = pl.BlockSpec(memory_space=pl.ANY)
+    vmem = pl.BlockSpec(memory_space=pltpu.VMEM)
+    f32, i32, bf16 = jnp.float32, jnp.int32, jnp.bfloat16
+    return pl.pallas_call(
+        kernel,
+        out_shape=(jax.ShapeDtypeStruct((1, NI, NV, OWN), f32), jax.ShapeDtypeStruct((8, 128), i32)),
+        in_specs=[any_space] * 8,
+        out_specs=(vmem, vmem),
+        scratch_shapes=[
+            pltpu.VMEM((NI, NV, OWN), f32),
+            pltpu.VMEM((NOFF, NV, OWN), f32),
+            pltpu.VMEM((NOFF, OWN), i32),
+            pltpu.VMEM((NV, NV, OWN), f32),
+            pltpu.VMEM((4, 10, 10, OWN), f32),
+            pltpu.VMEM((NV, NIF), f32),
+            pltpu.VMEM((ROWS, 2, 1, NIF), i32),
+            pltpu.VMEM((3200, 128), f32),
+            pltpu.VMEM((800, 128), f32),
+            pltpu.VMEM((48, 128), f32),
+            pltpu.VMEM((NOFF, 8, 128), i32),
+            pltpu.VMEM((384, 128), f32),
+            pltpu.VMEM((384, 128), f32),
+            pltpu.VMEM((384, 128), f32),
+            pltpu.VMEM((HALO_ROWS, 128), f32),
+            pltpu.VMEM((HALO_ROWS, 128), f32),
+            pltpu.VMEM((HALO_ROWS, 128), f32),
+            pltpu.VMEM((HALO_ROWS, 128), f32),
+            pltpu.VMEM((NS, NIF), f32),
+            pltpu.VMEM((4 * NS, 2 * OWN), bf16),
+            pltpu.VMEM((256, 2 * OWN), bf16),
+            pltpu.VMEM((CAP * NS, 1024), bf16),
+            pltpu.VMEM((4 * NS, 128), f32),
+            pltpu.VMEM((NS, 4, 128), f32),
+            pltpu.VMEM((NS, 4, 128), f32),
+            pltpu.SemaphoreType.DMA((8,)),
+            pltpu.SemaphoreType.DMA((ROWS,)),
+            pltpu.SemaphoreType.DMA((ROWS,)),
+            pltpu.SemaphoreType.DMA((2,)),
+            pltpu.SemaphoreType.DMA((2,)),
+            pltpu.SemaphoreType.DMA,
+            pltpu.SemaphoreType.DMA,
+        ],
+        compiler_params=pltpu.CompilerParams(
+            collective_id=0, has_side_effects=True, vmem_limit_bytes=40 * 1024 * 1024),
+    )(*args)
 
 
 def with_halo(block, sides, width):
@@ -66,7 +524,7 @@
     return accumulated
 
 
-def on_device(
+def general(
     right_side, coupling, offsets, block_mean, block_wave, donor_cells, receiver_cells, inlet_gain
 ):
     space_rank = lax.axis_index("space")
@@ -105,6 +563,11 @@
     return state_field[None]
 
 
+def on_device(*args):
+    result, flag = fast(*args)
+    return lax.cond(flag[0, 0] > 0, lambda: general(*args), lambda: result)
+
+
 def solution(mesh):
     return jax.shard_map(
         on_device,

time: 1420 us -> 67.6 us (0.05); the launches traced: 1400 us -> 67.5 us
  waiting for transfers between devices: 642 us -> 0 us
  other arithmetic: 354 us -> 0 us
  local copies, waits for them, and re-layouts: 324 us -> 2.85 us
  starting transfers between devices: 52.5 us -> 0 us
  Pallas kernels: 0 us -> 50.5 us
    psum x3 -> x0, waiting for transfers between devices: 599 us -> none  [on_device(): summed = lax.psum(outgoing, 'space')]
    scatter-add x4 -> x0, other arithmetic: 302 us -> none  [on_device(): jnp.zeros_like(source_base).at[:, :, receiver_clip].add(inflow)]
    gather x99 -> x0, local copies, waits for them, and re-layouts: 275 us -> none  [the longest x96 248 us: neighbor_sum(): neighbor_vals = jnp.take(padded, cell_base + offsets[neighbor], axis=2)]
    ppermute x19 -> x0, starting transfers between devices: 52.4 us -> none  [the longest x8 28.9 us: with_halo(): lax.ppermute(lax.slice_in_dim(block, block.shape[dim] - width, None, axis...]
    pallas_call x0 -> x1, Pallas kernels: none -> 50.5 us  [fast(): pl.pallas_call(kernel, out_shape=(jax.ShapeDtypeStruct((1, NI, NV, OWN),...]
    ppermute x19 -> x0, waiting for transfers between devices: 42.9 us -> none  [the longest x8 23 us: with_halo(): lax.ppermute(lax.slice_in_dim(block, 0, width, axis=dim), axis, backward)]
    mul x10 -> x0, other arithmetic: 29.2 us -> none  [the longest x3 28.2 us: on_device(): jnp.take(state_field, donor_clip, axis=2) * donor_inside[None, None, :]]
  transfers between devices with their start and end apart: 22 -> 0, of which waited for: 14 -> 0; matrix products, arithmetic and copies ran while one was open for 0% -> 0% of each run, Pallas kernels for 0% -> 0%
where the time goes in v1:
time: 67.6 us; the launch traced here: 67.5 us
  Pallas kernels  50.5 us (75%)
  between operations  14.2 us (21%)
  local copies, waits for them, and re-layouts  2.85 us (4%)
    pallas_call x1, Pallas kernels, fast(): pl.pallas_call(kernel, out_shape=(jax.ShapeDtypeStruct((1, NI, NV, OWN),...  50.5 us
    unnamed x22, local copies, waits for them, and re-layouts  1.6 us

profile of v1, /device:TPU:25, one launch (start us, length us, event | category | flops | bytes accessed | tf_op | source)
XLA Modules:
  0.0 67.5 jit_solution(4232050189894786058)
XLA Ops:
  6.5 0.0 copy-start
  6.5 0.0 copy-start.17
  6.5 0.0 copy-start.23
  6.5 0.0 copy-start.1
  6.5 0.0 copy-start.24
  6.5 0.0 copy-start.42
  6.6 0.0 copy-start.55
  6.6 0.0 copy-start.56
  6.6 1.5 %copy.441.bw_h = f32[1,4,10,10,512]{4,3,2,1,0:T(8,128)S(1)} copy(f32[1,4,10,10,512]{4,1,3,2,0:T(4,128)} %param.18) | data formatting | bytes 1638400 | tf_op args[4]
  8.1 0.0 copy-done.17
  8.1 0.0 copy-done.23
  8.2 0.0 copy-done.1
  8.2 0.0 copy-done.24
  8.2 0.0 copy-done.42
  8.2 0.0 copy-done.55
  8.3 0.0 copy-done.56
  8.3 50.5 %shard_map.84 = (f32[1,9,5,512]{3,2,1,0:T(8,128)S(1)}, s32[8,128]{1,0:T(8,128)S(1)}) custom-call(f32[1,9,5,512]{3,2,1,0:T(8,128)S(1)} %copy.437.rhs_h, f32[1,6,5,512]{3,2,1,0:T(8,128)S(1)} %copy.438.cpl_h, s32[1,6,512]{2,1,0:T(8,128)S(1)} %copy.439.off_h, f32[1,5,5,512]{3,2,1,0:T(8,128)S(1)} %copy.440.bm_h, f32[1,4,10,10,512]{4,3,2,1,0:T(8,128)S(1)} %copy.441.bw_h, ...), custom_call_target="tpu_custom_call" | custom-call | tf_op jit(solution)/shard_map/pallas_call | solution.py:429
  58.7 0.5 slice.118
  59.9 0.0 copy-done
  59.9 0.7 %conditional.1 = (f32[1,9,5,512]{3,0,2,1:T(1,128)}) conditional(s32[]{:T(128)} %bitcast.91, f32[1,9,5,512]{3,2,1,0:T(8,128)S(1)} %get-tuple-element.38, (f32[1,5,5,512]{3,0,2,1:T(1,128)S(1)}, f32[1,9,5,512]{3,0,2,1:T(1,128)S(1)}, s32[1,1024]{1,0:T(1,128)S(1)}, f32[1,5,1024]{2,0,1:T(1,128)S(1)}, f32[1,6,5,512]{3,0,2,1:T(1,128)S(1)}, ...), branch_computations={%region_0.0_spmd, %region_1.35_spmd} | conditional | flops 69742800 | bytes 104590960 | solution.py:568
  59.9 0.7 %copy.475 = f32[1,9,5,512]{3,0,2,1:T(1,128)} copy(f32[1,9,5,512]{3,2,1,0:T(8,128)S(1)} %param) | data formatting | bytes 184320 | tf_op jit(solution)/shard_map/cond
  (5 shorter events, 0.1 us)
Async XLA Ops:
  6.5 53.4 %copy-start = (f32[1,4,10,10,512]{4,1,3,2,0:T(4,128)S(1)}, f32[1,4,10,10,512]{4,1,3,2,0:T(4,128)}, u32[]{:S(2)}) copy-start(f32[1,4,10,10,512]{4,1,3,2,0:T(4,128)} %param.18) | copy-start | bytes 2457604
  6.5 1.6 %copy-start.17 = (f32[1,9,5,512]{3,0,2,1:T(1,128)S(1)}, f32[1,9,5,512]{3,0,2,1:T(1,128)}, u32[]{:S(2)}) copy-start(f32[1,9,5,512]{3,0,2,1:T(1,128)} %param.14) | copy-start | bytes 276484
  6.5 1.6 %copy-start.23 = (f32[1,6,5,512]{3,0,2,1:T(1,128)S(1)}, f32[1,6,5,512]{3,0,2,1:T(1,128)}, u32[]{:S(2)}) copy-start(f32[1,6,5,512]{3,0,2,1:T(1,128)} %param.15) | copy-start | bytes 184324
  6.5 1.6 %copy-start.1 = (f32[1,5,5,512]{3,0,2,1:T(1,128)S(1)}, f32[1,5,5,512]{3,0,2,1:T(1,128)}, u32[]{:S(2)}) copy-start(f32[1,5,5,512]{3,0,2,1:T(1,128)} %param.17) | copy-start | bytes 153604
  6.5 1.7 %copy-start.24 = (f32[1,5,1024]{2,0,1:T(1,128)S(1)}, f32[1,5,1024]{2,0,1:T(1,128)}, u32[]{:S(2)}) copy-start(f32[1,5,1024]{2,0,1:T(1,128)} %param.21) | copy-start | bytes 61444
  6.5 1.7 %copy-start.42 = (s32[1,6,512]{2,0,1:T(1,128)S(1)}, s32[1,6,512]{2,0,1:T(1,128)}, u32[]{:S(2)}) copy-start(s32[1,6,512]{2,0,1:T(1,128)} %param.16) | copy-start | bytes 36868
  6.6 1.7 %copy-start.55 = (s32[1,1024]{1,0:T(1,128)S(1)}, s32[1,1024]{1,0:T(1,128)}, u32[]{:S(2)}) copy-start(s32[1,1024]{1,0:T(1,128)} %don_h.1) | copy-start | bytes 12292
  6.6 1.7 %copy-start.56 = (s32[1,1024]{1,0:T(1,128)S(1)}, s32[1,1024]{1,0:T(1,128)}, u32[]{:S(2)}) copy-start(s32[1,1024]{1,0:T(1,128)} %rec_h.1) | copy-start | bytes 12292

commit v2 on v1

v2 whole, which is shorter than its diff:
```python
import functools
import math

import jax
import jax.numpy as jnp
import numpy as np
from jax import lax
from jax.experimental import pallas as pl
from jax.experimental.pallas import tpu as pltpu
from jax.sharding import PartitionSpec as P

NI = 9
NV = 5
NF = NI * NV
NOFF = 6
HALO = 16
SWEEPS = 2
NIF = 1024
ROWS = 4
NS = 64
GROUP = 8
OWN = 512
EDGE = 32
CAP = 8
MESH = pl.DeviceIdType.MESH

HALO_ROWS = 136
AT_BASE = 104
BASE = ((0, 25), (25, 30), (55, 45), (100, 6))


def field_row(f):
    return (f if f < 25 else f + 7) * 8


def spectral_numbers():
    n = np.arange(NI, dtype=np.float64)
    table = [np.full(NI, 1.0 / math.sqrt(NI))]
    for k in range(1, (NI - 1) // 2 + 1):
        table.append(math.sqrt(2.0 / NI) * np.cos(2.0 * math.pi * k * n / NI))
        table.append(math.sqrt(2.0 / NI) * np.sin(2.0 * math.pi * k * n / NI))
    return np.stack(table).astype(np.float32)


def kernel(
    rhs_h, cpl_h, off_h, bm_h, bw_h, don_h, rec_h, gain_h,
    out_ref, flag_ref,
    rhs_v, cpl_v, off_v, bm_v, bw_v, gain_v, idx_v,
    wave_w, base_w, edge_s, lane_w, src_w, x_w, y_w,
    send_left, send_right, from_left, from_right,
    code_s, sel_s, xr_s, wr_s, gpk_s, msg_s, got_s,
    in_sem, idx_send, idx_recv, edge_send, edge_recv, msg_send, msg_recv, ready,
):
    r = lax.axis_index("row")
    s = lax.axis_index("space")

    z, p = s // GROUP, s % GROUP

    bar = pltpu.get_barrier_semaphore()

    def greet(row, t):
        pl.semaphore_signal(bar, inc=1, device_id=(row, t), device_id_type=MESH)

    @pl.when(r < ROWS - 1)
    def _():
        for j in range(GROUP):
            greet(r + 1, j * GROUP + p)

    @pl.when(r > 0)
    def _():
        for j in range(GROUP):
            greet(r - 1, j * GROUP + p)

    for j in range(1, GROUP):
        greet(r, z * GROUP + lax.rem(p + j, GROUP))

    @pl.when((p == 0) & (s > 0))
    def _():
        greet(r, s - 1)

    @pl.when((p == GROUP - 1) & (s < NS - 1))
    def _():
        greet(r, s + 1)

    for row in range(ROWS):
        @pl.when((row > r + 1) | (row < r - 1))
        def _():
            greet(row, s)

    loads = [
        pltpu.make_async_copy(bw_h, bw_v, in_sem.at[0]),
        pltpu.make_async_copy(bm_h, bm_v, in_sem.at[1]),
        pltpu.make_async_copy(cpl_h, cpl_v, in_sem.at[2]),
        pltpu.make_async_copy(rhs_h, rhs_v, in_sem.at[3]),
        pltpu.make_async_copy(off_h, off_v, in_sem.at[4]),
        pltpu.make_async_copy(gain_h, gain_v, in_sem.at[5]),
        pltpu.make_async_copy(don_h, idx_v.at[r, 0], in_sem.at[6]),
        pltpu.make_async_copy(rec_h, idx_v.at[r, 1], in_sem.at[7]),
    ]
    for c in loads:
        c.start()

    lane8 = lax.broadcasted_iota(jnp.int32, (8, 128), 1)

    def to_windows(tiles, dst, row):
        n = tiles[0].shape[0]
        lane = lane8[:n]
        up = [pltpu.roll(t, 32, 1) for t in tiles]
        down = [pltpu.roll(t, 96, 1) for t in tiles]
        for m in range(4):
            even = up[m] if m == 0 else jnp.where(lane < 32, up[m - 1], up[m])
            odd = down[m] if m == 3 else jnp.where(lane < 96, down[m], down[m + 1])
            dst[pl.ds(row + 2 * m, n, stride=8), :] = even
            dst[pl.ds(row + 2 * m + 1, n, stride=8), :] = odd

    def pack(firsts, lasts, row):
        n = firsts[0].shape[0]
        lane = lane8[:n]
        left = firsts[0]
        right = pltpu.roll(lasts[0], 32, 1)
        for e in range(1, len(firsts)):
            left = jnp.where(lane >= 32 * e, pltpu.roll(firsts[e], 32 * e, 1), left)
            moved = lasts[e] if e == 3 else pltpu.roll(lasts[e], (32 * e + 32) % 128, 1)
            right = jnp.where(lane >= 32 * e, moved, right)
        send_left[pl.ds(row, n), :] = left
        send_right[pl.ds(row, n), :] = right

    loads[0].wait()

    def wave_units(first, count, row):
        firsts, lasts = [], []
        for e in range(count):
            tiles = [
                jnp.concatenate([bw_v[2 * (first + e) + i, :, pl.ds(128 * m, 128)] for i in range(2)], axis=0)
                for m in range(4)
            ]
            to_windows(tiles, wave_w, (first + e) * 64)
            firsts.append(tiles[0])
            lasts.append(tiles[3])
        pack(firsts, lasts, row)

    def wave_rows(p, c):
        wave_units(4 * p, 4, 8 * p)
        return c

    lax.fori_loop(0, 12, wave_rows, 0)
    wave_units(48, 2, 96)

    for c in loads[1:5]:
        c.wait()
    lane4 = lane8[:4]
    row4 = lax.broadcasted_iota(jnp.int32, (4, 128), 0)
    for ref, (first, count) in zip((bm_v, cpl_v, rhs_v, off_v), BASE):
        def base_rows(i, c, ref=ref, first=first):
            tile = ref[i].astype(jnp.float32)
            up = pltpu.roll(tile, 32, 1)
            down = pltpu.roll(tile, 96, 1)
            at = (first + i) * 8
            base_w[pl.ds(at, 4, stride=2), :] = jnp.where(lane4 < 32, pltpu.roll(up, 1, 0), up)
            base_w[pl.ds(at + 1, 4, stride=2), :] = jnp.where(lane4 < 96, down, pltpu.roll(down, 3, 0))
            edge_s[0, pl.ds(first + i, 1), :] = tile[0:1]
            edge_s[1, pl.ds(first + i, 1), :] = tile[3:4]
            return c
        lax.fori_loop(0, count, base_rows, 0, unroll=5 if count % 5 == 0 else 6)
    edge_s[:, pl.ds(106, 22), :] = jnp.zeros((2, 22, 128), jnp.float32)
    for q in range(4):
        pack(
            [edge_s[0, pl.ds(32 * e + 8 * q, 8), :] for e in range(4)],
            [edge_s[1, pl.ds(32 * e + 8 * q, 8), :] for e in range(4)], AT_BASE + 8 * q)
    for c in loads[5:]:
        c.wait()
    xr_s[...] = jnp.zeros(xr_s.shape, jnp.bfloat16)
    for ref in (src_w, x_w):
        ref[pl.ds(200, 56), :] = jnp.zeros((56, 128), jnp.float32)
        ref[pl.ds(416, 96), :] = jnp.zeros((96, 128), jnp.float32)

    @pl.when(s == 0)
    def _():
        from_left[...] = jnp.zeros(from_left.shape, jnp.float32)

    @pl.when(s == NS - 1)
    def _():
        from_right[...] = jnp.zeros(from_right.shape, jnp.float32)

    def one_if(condition):
        return jnp.where(condition, 1, 0)

    here = GROUP * (one_if(r > 0) + one_if(r < ROWS - 1)) + GROUP - 1
    here = here + one_if((p == 0) & (s > 0)) + one_if((p == GROUP - 1) & (s < NS - 1))
    here = here + 1 + one_if(r == 0) + one_if(r == ROWS - 1)
    pl.semaphore_wait(bar, here)

    right = pltpu.make_async_remote_copy(
        send_right, from_left, edge_send.at[0], edge_recv.at[0],
        device_id=(r, lax.rem(s + 1, NS)), device_id_type=MESH)
    left = pltpu.make_async_remote_copy(
        send_left, from_right, edge_send.at[1], edge_recv.at[1],
        device_id=(r, lax.rem(s + NS - 1, NS)), device_id_type=MESH)

    @pl.when(s < NS - 1)
    def _():
        right.start()

    @pl.when(s > 0)
    def _():
        left.start()

    index_copies = [
        pltpu.make_async_remote_copy(
            idx_v.at[r], idx_v.at[r], idx_send.at[d], idx_recv.at[d],
            device_id=(lax.rem(r + d, ROWS), s), device_id_type=MESH)
        for d in range(1, ROWS)
    ]
    for c in index_copies:
        c.start()

    @pl.when(r > 0)
    def _():
        for j in range(GROUP):
            pl.semaphore_signal(ready, inc=1, device_id=(r - 1, j * GROUP + p), device_id_type=MESH)

    dev64 = lax.broadcasted_iota(jnp.int32, (NS, 1), 0)
    tri = (lax.broadcasted_iota(jnp.int32, (128, 128), 0) <= lax.broadcasted_iota(jnp.int32, (128, 128), 1))
    tri = tri.astype(jnp.float32).astype(jnp.bfloat16)

    def order(mask):
        before = jnp.zeros((NS, 1), jnp.float32)
        for b in range(NIF // 128):
            m = mask[:, 128 * b:128 * b + 128]
            upto = jnp.dot(m.astype(jnp.bfloat16), tri, preferred_element_type=jnp.float32)
            code_s[:, pl.ds(128 * b, 128)] = jnp.where(m > 0.5, before + upto - 1.0, -1.0)
            before = before + jnp.sum(m, axis=1, keepdims=True)

    def pick(k, value):
        return jnp.sum(jnp.where(code_s[...] == float(k), value, 0.0), axis=1, keepdims=True)

    def in_block(cells, device):
        low = device * OWN
        return (cells >= low) & (cells < low + OWN)

    def in_windows(cells, device):
        low = device * OWN - EDGE
        return (cells >= low) & (cells < low + OWN + 2 * EDGE)

    @pl.when(r < ROWS - 1)
    def _():
        index_copies[2].wait_recv()
        donor = idx_v[r, 0]
        receiver = idx_v[r + 1, 1]
        order((in_block(donor, s) & in_windows(receiver, dev64)).astype(jnp.float32))
        place = (donor - s * OWN + 1).astype(jnp.float32)
        cell = lax.broadcasted_iota(jnp.int32, (NS, OWN), 1).astype(jnp.float32) + 1.0
        for k in range(CAP):
            hit = (pick(k, place) == cell).astype(jnp.float32).astype(jnp.bfloat16)
            sel_s[pl.ds(k * NS, NS), :] = hit

    @pl.when(r > 0)
    def _():
        index_copies[0].wait_recv()
        donor = idx_v[r - 1, 0]
        receiver = idx_v[r, 1]
        order((in_block(donor, dev64) & in_windows(receiver, s)).astype(jnp.float32))
        place = (receiver - s * OWN + EDGE + 1).astype(jnp.float32)
        position = lax.broadcasted_iota(jnp.int32, (NS, 1024), 1)
        cell = ((position // 128) * 64 + position % 128 + 1).astype(jnp.float32)
        lane = lax.broadcasted_iota(jnp.int32, (1, 128), 1)
        field = lane % 32
        for k in range(CAP):
            hit = (pick(k, place) == cell).astype(jnp.float32).astype(jnp.bfloat16)
            wr_s[pl.ds(k * NS, NS), :] = hit
        for k in range(2):
            rows = jnp.zeros((NS, 128), jnp.float32)
            for v in range(NV):
                for g in range(4):
                    mine = (field % NV == v) & (field < 25) & (lane // 32 == g)
                    rows = rows + jnp.where(mine, pick(2 * g + k, gain_v[v]), 0.0)
            gpk_s[pl.ds(k * NS, NS), :] = rows

    @pl.when(s > 0)
    def _():
        right.wait_recv()

    @pl.when(s < NS - 1)
    def _():
        left.wait_recv()

    def merge(dst, row, n, src_row, e):
        lane = lane8[:n]
        low = from_left[pl.ds(src_row, n), :]
        low = low if e == 0 else pltpu.roll(low, 128 - 32 * e, 1)
        high = from_right[pl.ds(src_row, n), :]
        high = high if e == 3 else pltpu.roll(high, 96 - 32 * e, 1)
        at = pl.ds(row, n, stride=8)
        dst[at, :] = jnp.where(lane < 32, low, dst[at, :])
        at = pl.ds(row + 7, n, stride=8)
        dst[at, :] = jnp.where(lane >= 96, high, dst[at, :])

    def wave_edges(p, c):
        for e in range(4):
            merge(wave_w, (4 * p + e) * 64, 8, 8 * p, e)
        return c

    lax.fori_loop(0, 12, wave_edges, 0)
    for e in range(2):
        merge(wave_w, (48 + e) * 64, 8, 96, e)
    for e in range(4):
        for q in range(4 if e < 3 else 2):
            merge(base_w, (32 * e + 8 * q) * 8, 8, AT_BASE + 8 * q, e)

    for j in range(NOFF):
        at = lane8 + base_w[pl.ds((100 + j) * 8, 8), :].astype(jnp.int32)
        lane_w[j] = jnp.clip(at, 0, 127)

    table = spectral_numbers()
    for v in range(NV):
        parts = [base_w[pl.ds((55 + n * NV + v) * 8, 8), :] for n in range(NI)]
        for m in range(NI):
            total = float(table[m, 0]) * parts[0]
            for n in range(1, NI):
                total = total + float(table[m, n]) * parts[n]
            src_w[pl.ds(field_row(m * NV + v), 8), :] = total

    def inflow(h):
        pltpu.make_async_remote_copy(
            msg_s.at[h], got_s.at[h], msg_send.at[h], msg_recv.at[h],
            device_id=(r - 1, s), device_id_type=MESH).wait_recv()
        rows = jnp.concatenate([got_s[h, :, k, :] for k in range(2)], axis=0) * gpk_s[...]
        turned = rows.T
        both = jnp.concatenate([turned[32 * g:32 * g + 32] for g in range(4)], axis=1)
        high = both.astype(jnp.bfloat16)
        low = (both - high.astype(jnp.float32)).astype(jnp.bfloat16)
        added = jnp.dot(jnp.concatenate([high, low], axis=0), wr_s[...], preferred_element_type=jnp.float32)
        added = added[:32] + added[32:]
        for a in range(4 - h):
            for j in range(8):
                at = pl.ds(h * 256 + a * 64 + j, 8, stride=8)
                src_w[at, :] = src_w[at, :] - added[8 * a:8 * a + 8, 128 * j:128 * j + 128]

    def relax(row, count, entry):
        source = [src_w[pl.ds(row + f * 8, 8), :] for f in range(count)]

        def solve(values):
            result = []
            for f in range(count):
                total = None
                for g in range(count):
                    term = entry(f, g) * values[g]
                    total = term if total is None else total + term
                result.append(total)
            return result

        x = solve(source)
        for _ in range(SWEEPS):
            rest = list(source)
            for j in range(NOFF):
                at = lane_w[j]
                for f in range(count):
                    moved = jnp.take_along_axis(x[f], at, axis=1, mode="promise_in_bounds")
                    rest[f] = rest[f] - base_w[pl.ds((25 + j * NV + f % NV) * 8, 8), :] * moved
            x = solve(rest)
        for f in range(count):
            x_w[pl.ds(row + f * 8, 8), :] = x[f]

    def harmonic(k, c):
        row = jnp.where(k < 2, 40 + 80 * k, 256 + 80 * (k - 2))
        relax(row, 10, lambda f, g: wave_w[pl.ds((f * 10 + g) * 32 + k * 8, 8), :])
        return c

    def relax_half(h):
        if h == 0:
            relax(0, NV, lambda f, g: base_w[pl.ds((f * NV + g) * 8, 8), :])
        lax.fori_loop(2 * h, 2 * h + 2, harmonic, 0)

    def own_tile(ref, row, n, m):
        lane = lane8[:n]
        even = ref[pl.ds(row + 2 * m, n, stride=8), :]
        odd = ref[pl.ds(row + 2 * m + 1, n, stride=8), :]
        return jnp.where(lane < 64, pltpu.roll(even, 96, 1), pltpu.roll(odd, 32, 1))

    def donate(h):
        for a in range(2):
            for m in range(4):
                tile = jnp.concatenate(
                    [own_tile(x_w, h * 256 + (2 * a + i) * 64, 8, m) for i in range(2)], axis=0)
                high = tile.astype(jnp.bfloat16)
                low = (tile - high.astype(jnp.float32)).astype(jnp.bfloat16)
                xr_s[pl.ds(16 * a, 16), pl.ds(128 * m, 128)] = high
                xr_s[pl.ds(128 + 16 * a, 16), pl.ds(128 * m, 128)] = low
        values = lax.dot_general(
            sel_s[...], xr_s[...], (((1,), (1,)), ((), ())), preferred_element_type=jnp.float32)
        values = values[:, :128] + values[:, 128:]
        for k in range(2):
            rows = values[k * NS:(k + 1) * NS]
            for g in range(1, 4):
                at = (2 * g + k) * NS
                rows = rows + pltpu.roll(values[at:at + NS], 32 * g, 1)
            msg_s[h, :, k, :] = rows
        if h == 0:
            pl.semaphore_wait(ready, GROUP)

        def send(j, c):
            t = lax.rem(s + 36 + j, NS)
            pltpu.make_async_remote_copy(
                msg_s.at[h, t], got_s.at[h, s], msg_send.at[h], msg_recv.at[h],
                device_id=(r + 1, t), device_id_type=MESH).start()
            return c

        lax.fori_loop(0, NS, send, 0, unroll=8)

    for h in range(2):
        @pl.when(r > 0)
        def _():
            inflow(h)

        relax_half(h)

        @pl.when(r < ROWS - 1)
        def _():
            donate(h)

    for v in range(NV):
        parts = [x_w[pl.ds(field_row(m * NV + v), 8), :] for m in range(NI)]
        for n in range(NI):
            total = float(table[0, n]) * parts[0]
            for m in range(1, NI):
                total = total + float(table[m, n]) * parts[m]
            y_w[pl.ds((n * NV + v) * 8, 8), :] = total
    def out_rows(i, c):
        even = y_w[pl.ds(i * 8, 4, stride=2), :]
        odd = y_w[pl.ds(i * 8 + 1, 4, stride=2), :]
        out_ref[i] = jnp.where(lane4 < 64, pltpu.roll(even, 96, 1), pltpu.roll(odd, 32, 1))
        return c

    lax.fori_loop(0, NF, out_rows, 0, unroll=5)

    @pl.when(r == ROWS - 1)
    def _():
        index_copies[2].wait_recv()

    @pl.when(r == 0)
    def _():
        index_copies[0].wait_recv()

    index_copies[1].wait_recv()
    for c in index_copies:
        c.wait_send()
    most = jnp.zeros((NS, NS), jnp.float32)
    for row in range(ROWS - 1):
        gives = in_block(idx_v[row, 0], dev64).astype(jnp.float32).astype(jnp.bfloat16)
        takes = in_windows(idx_v[row + 1, 1], dev64).astype(jnp.float32).astype(jnp.bfloat16)
        count = lax.dot_general(gives, takes, (((1,), (1,)), ((), ())), preferred_element_type=jnp.float32)
        most = jnp.maximum(most, count)
    flag_ref[0, 0] = jnp.where(jnp.max(most) > CAP + 0.5, 1, 0)

    @pl.when(s < NS - 1)
    def _():
        right.wait_send()

    @pl.when(s > 0)
    def _():
        left.wait_send()

    @pl.when(r < ROWS - 1)
    def _():
        for h in range(2):
            pltpu.make_async_remote_copy(
                msg_s.at[h], got_s.at[h], msg_send.at[h], msg_recv.at[h],
                device_id=(r + 1, s), device_id_type=MESH).wait_send()


def fast(rhs, cpl, off, bm, bw, don, rec, gain):
    bw = jnp.transpose(bw, (0, 2, 3, 1, 4)).reshape(100, 4, OWN)
    rhs, cpl, off, bm = (a.reshape(-1, 4, 128) for a in (rhs, cpl, off, bm))
    gain = gain.reshape(NV, 1, NIF)
    any_space = pl.BlockSpec(memory_space=pl.ANY)
    vmem = pl.BlockSpec(memory_space=pltpu.VMEM)
    f32, i32, bf16 = jnp.float32, jnp.int32, jnp.bfloat16
    return pl.pallas_call(
        kernel,
        out_shape=(jax.ShapeDtypeStruct((NF, 4, 128), f32), jax.ShapeDtypeStruct((1, 1), i32)),
        in_specs=[any_space] * 8,
        out_specs=(vmem, pl.BlockSpec(memory_space=pltpu.SMEM)),
        scratch_shapes=[
            pltpu.VMEM((NF, 4, 128), f32),
            pltpu.VMEM((NOFF * NV, 4, 128), f32),
            pltpu.VMEM((NOFF, 4, 128), i32),
            pltpu.VMEM((NV * NV, 4, 128), f32),
            pltpu.VMEM((100, 4, OWN), f32),
            pltpu.VMEM((NV, 1, NIF), f32),
            pltpu.VMEM((ROWS, 2, 1, NIF), i32),
            pltpu.VMEM((3200, 128), f32),
            pltpu.VMEM((1024, 128), f32),
            pltpu.VMEM((2, 128, 128), f32),
            pltpu.VMEM((NOFF, 8, 128), i32),
            pltpu.VMEM((512, 128), f32),
            pltpu.VMEM((512, 128), f32),
            pltpu.VMEM((384, 128), f32),
            pltpu.VMEM((HALO_ROWS, 128), f32),
            pltpu.VMEM((HALO_ROWS, 128), f32),
            pltpu.VMEM((HALO_ROWS, 128), f32),
            pltpu.VMEM((HALO_ROWS, 128), f32),
            pltpu.VMEM((NS, NIF), f32),
            pltpu.VMEM((CAP * NS, OWN), bf16),
            pltpu.VMEM((256, OWN), bf16),
            pltpu.VMEM((CAP * NS, 1024), bf16),
            pltpu.VMEM((2 * NS, 128), f32),
            pltpu.VMEM((2, NS, 2, 128), f32),
            pltpu.VMEM((2, NS, 2, 128), f32),
            pltpu.SemaphoreType.DMA((8,)),
            pltpu.SemaphoreType.DMA((ROWS,)),
            pltpu.SemaphoreType.DMA((ROWS,)),
            pltpu.SemaphoreType.DMA((2,)),
            pltpu.SemaphoreType.DMA((2,)),
            pltpu.SemaphoreType.DMA((2,)),
            pltpu.SemaphoreType.DMA((2,)),
            pltpu.SemaphoreType.REGULAR,
        ],
        compiler_params=pltpu.CompilerParams(
            collective_id=0, has_side_effects=True, vmem_limit_bytes=40 * 1024 * 1024),
    )(rhs, cpl, off, bm, bw, don, rec, gain)


def with_halo(block, sides, width):
    for axis, dim in sides:
        count = lax.axis_size(axis)
        forward = [(i, i + 1) for i in range(count - 1)]
        backward = [(target, source) for source, target in forward]
        low = lax.ppermute(
            lax.slice_in_dim(block, block.shape[dim] - width, None, axis=dim), axis, forward
        )
        high = lax.ppermute(lax.slice_in_dim(block, 0, width, axis=dim), axis, backward)
        block = jnp.concatenate([low, block, high], axis=dim)
    return block


def from_behind(value, axis, steps):
    count = lax.axis_size(axis)
    first, last = (max(0, -steps), min(count, count - steps))
    return lax.ppermute(value, axis, [(source, source + steps) for source in range(first, last)])


def sum_over(value, axis):
    count = lax.axis_size(axis)
    step = 1
    while step < count:
        value = value + lax.ppermute(value, axis, [(i, i ^ step) for i in range(count)])
        step *= 2
    return value


def spectral_table(instances):
    position = jnp.arange(instances).astype(jnp.float32)
    harmonic = jnp.arange(1, (instances - 1) // 2 + 1).astype(jnp.float32)
    phase_angle = 2.0 * math.pi / instances * harmonic[:, None] * position[None, :]
    weight = math.sqrt(2.0 / instances)
    wave_rows = jnp.stack(
        [weight * jnp.cos(phase_angle), weight * jnp.sin(phase_angle)], axis=1
    ).reshape(-1, instances)
    mean_row = jnp.full((1, instances), 1.0 / math.sqrt(instances), jnp.float32)
    return jnp.concatenate([mean_row, wave_rows], axis=0)


def invert_blocks(values, block_mean, block_wave, spectral):
    spectral_modes = jnp.einsum("kn,nvc->kvc", spectral, values, precision=lax.Precision.HIGHEST)
    variables = spectral_modes.shape[1]
    harmonics = (spectral_modes.shape[0] - 1) // 2
    steady = jnp.sum(block_mean * spectral_modes[0][None, :, :], axis=1)
    paired = spectral_modes[1:].reshape(harmonics, 2 * variables, spectral_modes.shape[2])
    paired = jnp.sum(block_wave * paired[:, None, :, :], axis=2)
    joined = jnp.concatenate(
        [steady[None], paired.reshape(2 * harmonics, variables, spectral_modes.shape[2])], axis=0
    )
    return jnp.einsum("kn,kvc->nvc", spectral, joined, precision=lax.Precision.HIGHEST)


def neighbor_sum(padded, offsets, coupling, reach_cells):
    cell_count = offsets.shape[1]
    cell_base = jnp.arange(cell_count, dtype=jnp.int32) + reach_cells
    accumulated = jnp.zeros((padded.shape[0], padded.shape[1], cell_count), jnp.float32)
    for neighbor in range(offsets.shape[0]):
        neighbor_vals = jnp.take(padded, cell_base + offsets[neighbor], axis=2)
        accumulated = accumulated + coupling[neighbor][None, :, :] * neighbor_vals
    return accumulated


def general(
    right_side, coupling, offsets, block_mean, block_wave, donor_cells, receiver_cells, inlet_gain
):
    space_rank = lax.axis_index("space")
    source_base = right_side[0]
    cell_count = source_base.shape[2]
    spectral = spectral_table(source_base.shape[0])
    first_cell = space_rank * cell_count
    mean_blocks = block_mean[0]
    wave_blocks = block_wave[0]

    def apply_inverse(values):
        return invert_blocks(values, mean_blocks, wave_blocks, spectral)

    donor_local = donor_cells[0] - first_cell
    donor_inside = ((donor_local >= 0) & (donor_local < cell_count)).astype(jnp.float32)
    donor_clip = jnp.clip(donor_local, 0, cell_count - 1)
    receiver_local = receiver_cells[0] - first_cell
    receiver_inside = ((receiver_local >= 0) & (receiver_local < cell_count)).astype(jnp.float32)
    receiver_clip = jnp.clip(receiver_local, 0, cell_count - 1)
    row_total = lax.axis_size("row")
    inlet_profile = jnp.zeros((NI, NV, NIF), jnp.float32)

    def row(_, carry):
        inlet_profile, _ = carry
        inflow = inlet_gain[0][None, :, :] * inlet_profile * receiver_inside[None, None, :]
        source = source_base - jnp.zeros_like(source_base).at[:, :, receiver_clip].add(inflow)

        def sweep(_, state):
            padded = with_halo(state, (("space", 2),), HALO)
            coupled = neighbor_sum(padded, offsets[0], coupling[0], HALO)
            return apply_inverse(source - coupled)

        state_field = lax.fori_loop(0, SWEEPS, sweep, apply_inverse(source))
        outgoing = jnp.take(state_field, donor_clip, axis=2) * donor_inside[None, None, :]
        return from_behind(sum_over(outgoing, "space"), "row", 1), state_field

    return lax.fori_loop(0, row_total, row, (inlet_profile, source_base))[1][None]


def on_device(*args):
    result, flag = fast(*args)
    return lax.cond(flag[0, 0] > 0, lambda: general(*args), lambda: jnp.where(flag[0, 0] > 1, 0.0, result).reshape(1, NI, NV, OWN))


def solution(mesh):
    return jax.shard_map(
        on_device,
        mesh=mesh,
        in_specs=(
            P("row", None, None, "space"),
            P("row", None, None, "space"),
            P("row", None, "space"),
            P("row", None, None, "space"),
            P("row", None, None, None, "space"),
            P("row", None),
            P("row", None),
            P("row", None, None),
        ),
        out_specs=P("row", None, None, "space"),
        check_vma=False,
    )
```

time: 67.6 us -> 46.7 us (0.69)
  between operations: 14.2 us -> 0.65 us
  Pallas kernels: 50.5 us -> 44.4 us
  local copies, waits for them, and re-layouts: 2.85 us -> 0.63 us
  loops' own time: 0.01 us -> 0.86 us
    pallas_call x1, Pallas kernels: 50.5 us -> 44.4 us  [fast(): pl.pallas_call(kernel, out_shape=(jax.ShapeDtypeStruct((NF, 4, 128), f32)...]
    unnamed x22 -> x2, local copies, waits for them, and re-layouts: 1.6 us -> 0.63 us
    another operation x1, loops' own time: 0.01 us -> 0.86 us  [on_device(): lax.cond(flag[0, 0] > 0, lambda: general(*args), lambda: jnp.where(flag[0...]
    cond x1 -> x0, local copies, waits for them, and re-layouts: 0.73 us -> none
where the time goes in v2:
time: 46.7 us; the launch traced here: 46.5 us
  Pallas kernels  44.4 us (95%)
  loops' own time  0.86 us (2%)
  between operations  0.65 us (1%)
  local copies, waits for them, and re-layouts  0.63 us (1%)
    pallas_call x1, Pallas kernels, fast(): pl.pallas_call(kernel, out_shape=(jax.ShapeDtypeStruct((NF, 4, 128), f32)...  44.4 us

profile of v2, /device:TPU:25, one launch (start us, length us, event | category | flops | bytes accessed | tf_op | source)
XLA Modules:
  0.0 46.5 jit_solution(8405328115700288937)
XLA Ops:
  0.0 44.4 %shard_map.84 = (f32[45,4,128]{2,1,0:T(4,128)S(1)}, s32[1,1]{1,0:T(1,128)}) custom-call(f32[45,4,128]{2,1,0:T(4,128)} %bitcast.196, f32[30,4,128]{2,1,0:T(4,128)} %bitcast.202, s32[6,4,128]{2,1,0:T(4,128)} %bitcast.209, f32[25,4,128]{2,1,0:T(4,128)} %bitcast.203, f32[100,4,512]{2,1,0:T(4,128)} %bitcast.193, s32[1,1024]{1,0:T(1,128)} %don_h.1, ...), custom_call_target="tpu_custom_call" | custom-call | tf_op jit(solution)/shard_map/pallas_call | solution.py:478
  45.0 0.9 %conditional.1 = (f32[1,9,5,512]{3,0,2,1:T(1,128)S(1)}) conditional(s32[]{:T(128)} %bitcast.51, (s32[1,1]{1,0:T(1,128)}, f32[45,4,128]{2,1,0:T(4,128)S(1)}) %tuple.20, (f32[1,9,5,512]{3,0,2,1:T(1,128)}, s32[1,1024]{1,0:T(1,128)}, f32[1,5,5,512]{3,0,2,1:T(1,128)}, f32[1,4,10,10,512]{4,1,3,2,0:T(4,128)}, s32[1,1024]{1,0:T(1,128)}, ...), branch_computations={%region_0.1_spmd, %region_1.12_spmd} | conditional | flops 11981840 | bytes 23738944 | solution.py:628
  45.9 0.0 copy-start.16
  45.9 0.6 %copy-done.16 = f32[1,9,5,512]{3,0,2,1:T(1,128)} copy-done((f32[1,9,5,512]{3,0,2,1:T(1,128)}, f32[1,9,5,512]{3,0,2,1:T(1,128)S(1)}, u32[]{:S(2)}) %copy-start.16) | copy-done | bytes 92184
  (1 shorter events, 0.0 us)
Async XLA Ops:
  45.9 0.6 %copy-start.16 = (f32[1,9,5,512]{3,0,2,1:T(1,128)}, f32[1,9,5,512]{3,0,2,1:T(1,128)S(1)}, u32[]{:S(2)}) copy-start(f32[1,9,5,512]{3,0,2,1:T(1,128)S(1)} %get-tuple-element.623) | copy-start | bytes 276484

commit v3 on v2

--- a/solution.py
+++ b/solution.py
@@ -26,7 +26,7 @@
 
 HALO_ROWS = 136
 AT_BASE = 104
-BASE = ((0, 25), (25, 30), (55, 45), (100, 6))
+AT_SOURCE = 512
 
 
 def field_row(f):
@@ -42,11 +42,47 @@
     return np.stack(table).astype(np.float32)
 
 
+def own_tile(ref, row, n, m):
+    lane = lax.broadcasted_iota(jnp.int32, (n, 128), 1)
+    even = ref[pl.ds(row + 2 * m, n, stride=8), :]
+    odd = ref[pl.ds(row + 2 * m + 1, n, stride=8), :]
+    return jnp.where(lane < 64, pltpu.roll(even, 96, 1), pltpu.roll(odd, 32, 1))
+
+
+def finish_kernel(x_w, out_ref, y_w):
+    lane4 = lax.broadcasted_iota(jnp.int32, (4, 128), 1)
+    table = spectral_numbers()
+    for v in range(NV):
+        parts = [x_w[pl.ds(field_row(m * NV + v), 8), :] for m in range(NI)]
+        for n in range(NI):
+            total = float(table[0, n]) * parts[0]
+            for m in range(1, NI):
+                total = total + float(table[m, n]) * parts[m]
+            y_w[pl.ds((n * NV + v) * 8, 8), :] = total
+
+    def out_rows(i, c):
+        even = y_w[pl.ds(i * 8, 4, stride=2), :]
+        odd = y_w[pl.ds(i * 8 + 1, 4, stride=2), :]
+        out_ref[i] = jnp.where(lane4 < 64, pltpu.roll(even, 96, 1), pltpu.roll(odd, 32, 1))
+        return c
+
+    lax.fori_loop(0, NF, out_rows, 0, unroll=9)
+
+
+def finish(modes):
+    return pl.pallas_call(
+        finish_kernel,
+        out_shape=jax.ShapeDtypeStruct((NF, 4, 128), jnp.float32),
+        scratch_shapes=[pltpu.VMEM((NF * 8, 128), jnp.float32)],
+        cost_estimate=pl.CostEstimate(flops=2 * NI * NF * 1024, bytes_accessed=500000, transcendentals=0),
+    )(modes).reshape(1, NI, NV, OWN)
+
+
 def kernel(
     rhs_h, cpl_h, off_h, bm_h, bw_h, don_h, rec_h, gain_h,
-    out_ref, flag_ref,
+    x_w, flag_ref,
     rhs_v, cpl_v, off_v, bm_v, bw_v, gain_v, idx_v,
-    wave_w, base_w, edge_s, lane_w, src_w, x_w, y_w,
+    wave_w, base_w, edge_s, lane_w,
     send_left, send_right, from_left, from_right,
     code_s, sel_s, xr_s, wr_s, gpk_s, msg_s, got_s,
     in_sem, idx_send, idx_recv, edge_send, edge_recv, msg_send, msg_recv, ready,
@@ -143,16 +179,26 @@
         wave_units(4 * p, 4, 8 * p)
         return c
 
-    lax.fori_loop(0, 12, wave_rows, 0)
+    lax.fori_loop(0, 12, wave_rows, 0, unroll=3)
     wave_units(48, 2, 96)
 
     for c in loads[1:5]:
         c.wait()
     lane4 = lane8[:4]
     row4 = lax.broadcasted_iota(jnp.int32, (4, 128), 0)
-    for ref, (first, count) in zip((bm_v, cpl_v, rhs_v, off_v), BASE):
-        def base_rows(i, c, ref=ref, first=first):
-            tile = ref[i].astype(jnp.float32)
+    table = spectral_numbers()
+    for v in range(NV):
+        parts = [rhs_v[n * NV + v] for n in range(NI)]
+        for m in range(NI):
+            total = float(table[m, 0]) * parts[0]
+            for n in range(1, NI):
+                total = total + float(table[m, n]) * parts[n]
+            rhs_v[m * NV + v] = total
+
+    for ref, skip, first, count in (
+            (bm_v, 0, 0, 25), (cpl_v, 0, 25, 30), (off_v, 0, 55, 6), (rhs_v, 0, 64, 25), (rhs_v, 25, 96, 20)):
+        def base_rows(i, c, ref=ref, skip=skip, first=first):
+            tile = ref[skip + i].astype(jnp.float32)
             up = pltpu.roll(tile, 32, 1)
             down = pltpu.roll(tile, 96, 1)
             at = (first + i) * 8
@@ -162,7 +208,9 @@
             edge_s[1, pl.ds(first + i, 1), :] = tile[3:4]
             return c
         lax.fori_loop(0, count, base_rows, 0, unroll=5 if count % 5 == 0 else 6)
-    edge_s[:, pl.ds(106, 22), :] = jnp.zeros((2, 22, 128), jnp.float32)
+    for first, count in ((61, 3), (89, 7), (116, 12)):
+        edge_s[:, pl.ds(first, count), :] = jnp.zeros((2, count, 128), jnp.float32)
+        base_w[pl.ds(first * 8, count * 8), :] = jnp.zeros((count * 8, 128), jnp.float32)
     for q in range(4):
         pack(
             [edge_s[0, pl.ds(32 * e + 8 * q, 8), :] for e in range(4)],
@@ -170,9 +218,8 @@
     for c in loads[5:]:
         c.wait()
     xr_s[...] = jnp.zeros(xr_s.shape, jnp.bfloat16)
-    for ref in (src_w, x_w):
-        ref[pl.ds(200, 56), :] = jnp.zeros((56, 128), jnp.float32)
-        ref[pl.ds(416, 96), :] = jnp.zeros((96, 128), jnp.float32)
+    x_w[pl.ds(200, 56), :] = jnp.zeros((56, 128), jnp.float32)
+    x_w[pl.ds(416, 96), :] = jnp.zeros((96, 128), jnp.float32)
 
     @pl.when(s == 0)
     def _():
@@ -190,6 +237,14 @@
     here = here + 1 + one_if(r == 0) + one_if(r == ROWS - 1)
     pl.semaphore_wait(bar, here)
 
+    def index_copy(d, part, sem):
+        at = idx_v.at[r] if part is None else idx_v.at[r, part]
+        return pltpu.make_async_remote_copy(
+            at, at, idx_send.at[sem], idx_recv.at[sem],
+            device_id=(lax.rem(r + d, ROWS), s), device_id_type=MESH)
+
+    index_copies = [index_copy(ROWS - 1, 1, 0), index_copy(1, None, 1), index_copy(2, None, 2), index_copy(ROWS - 1, 0, 3)]
+    index_copies[0].start()
     right = pltpu.make_async_remote_copy(
         send_right, from_left, edge_send.at[0], edge_recv.at[0],
         device_id=(r, lax.rem(s + 1, NS)), device_id_type=MESH)
@@ -205,13 +260,7 @@
     def _():
         left.start()
 
-    index_copies = [
-        pltpu.make_async_remote_copy(
-            idx_v.at[r], idx_v.at[r], idx_send.at[d], idx_recv.at[d],
-            device_id=(lax.rem(r + d, ROWS), s), device_id_type=MESH)
-        for d in range(1, ROWS)
-    ]
-    for c in index_copies:
+    for c in index_copies[1:]:
         c.start()
 
     @pl.when(r > 0)
@@ -244,7 +293,7 @@
 
     @pl.when(r < ROWS - 1)
     def _():
-        index_copies[2].wait_recv()
+        index_copies[0].wait_recv()
         donor = idx_v[r, 0]
         receiver = idx_v[r + 1, 1]
         order((in_block(donor, s) & in_windows(receiver, dev64)).astype(jnp.float32))
@@ -256,7 +305,7 @@
 
     @pl.when(r > 0)
     def _():
-        index_copies[0].wait_recv()
+        index_copies[1].wait_recv()
         donor = idx_v[r - 1, 0]
         receiver = idx_v[r, 1]
         order((in_block(donor, dev64) & in_windows(receiver, s)).astype(jnp.float32))
@@ -300,25 +349,16 @@
             merge(wave_w, (4 * p + e) * 64, 8, 8 * p, e)
         return c
 
-    lax.fori_loop(0, 12, wave_edges, 0)
+    lax.fori_loop(0, 12, wave_edges, 0, unroll=12)
     for e in range(2):
         merge(wave_w, (48 + e) * 64, 8, 96, e)
     for e in range(4):
-        for q in range(4 if e < 3 else 2):
+        for q in range(4 if e < 3 else 3):
             merge(base_w, (32 * e + 8 * q) * 8, 8, AT_BASE + 8 * q, e)
 
     for j in range(NOFF):
-        at = lane8 + base_w[pl.ds((100 + j) * 8, 8), :].astype(jnp.int32)
+        at = lane8 + base_w[pl.ds((55 + j) * 8, 8), :].astype(jnp.int32)
         lane_w[j] = jnp.clip(at, 0, 127)
-
-    table = spectral_numbers()
-    for v in range(NV):
-        parts = [base_w[pl.ds((55 + n * NV + v) * 8, 8), :] for n in range(NI)]
-        for m in range(NI):
-            total = float(table[m, 0]) * parts[0]
-            for n in range(1, NI):
-                total = total + float(table[m, n]) * parts[n]
-            src_w[pl.ds(field_row(m * NV + v), 8), :] = total
 
     def inflow(h):
         pltpu.make_async_remote_copy(
@@ -333,11 +373,11 @@
         added = added[:32] + added[32:]
         for a in range(4 - h):
             for j in range(8):
-                at = pl.ds(h * 256 + a * 64 + j, 8, stride=8)
-                src_w[at, :] = src_w[at, :] - added[8 * a:8 * a + 8, 128 * j:128 * j + 128]
+                at = pl.ds(AT_SOURCE + h * 256 + a * 64 + j, 8, stride=8)
+                base_w[at, :] = base_w[at, :] - added[8 * a:8 * a + 8, 128 * j:128 * j + 128]
 
     def relax(row, count, entry):
-        source = [src_w[pl.ds(row + f * 8, 8), :] for f in range(count)]
+        source = [base_w[pl.ds(AT_SOURCE + row + f * 8, 8), :] for f in range(count)]
 
         def solve(values):
             result = []
@@ -369,13 +409,7 @@
     def relax_half(h):
         if h == 0:
             relax(0, NV, lambda f, g: base_w[pl.ds((f * NV + g) * 8, 8), :])
-        lax.fori_loop(2 * h, 2 * h + 2, harmonic, 0)
-
-    def own_tile(ref, row, n, m):
-        lane = lane8[:n]
-        even = ref[pl.ds(row + 2 * m, n, stride=8), :]
-        odd = ref[pl.ds(row + 2 * m + 1, n, stride=8), :]
-        return jnp.where(lane < 64, pltpu.roll(even, 96, 1), pltpu.roll(odd, 32, 1))
+        lax.fori_loop(2 * h, 2 * h + 2, harmonic, 0, unroll=2)
 
     def donate(h):
         for a in range(2):
@@ -398,14 +432,13 @@
         if h == 0:
             pl.semaphore_wait(ready, GROUP)
 
-        def send(j, c):
-            t = lax.rem(s + 36 + j, NS)
-            pltpu.make_async_remote_copy(
-                msg_s.at[h, t], got_s.at[h, s], msg_send.at[h], msg_recv.at[h],
-                device_id=(r + 1, t), device_id_type=MESH).start()
-            return c
-
-        lax.fori_loop(0, NS, send, 0, unroll=8)
+        for d in (4, 3, 5, 2, 6, 1, 7, 0):
+            plane = lax.rem(z + d, GROUP) * GROUP
+            for j in range(GROUP):
+                t = plane + j
+                pltpu.make_async_remote_copy(
+                    msg_s.at[h, t], got_s.at[h, s], msg_send.at[h], msg_recv.at[h],
+                    device_id=(r + 1, t), device_id_type=MESH).start()
 
     for h in range(2):
         @pl.when(r > 0)
@@ -418,30 +451,16 @@
         def _():
             donate(h)
 
-    for v in range(NV):
-        parts = [x_w[pl.ds(field_row(m * NV + v), 8), :] for m in range(NI)]
-        for n in range(NI):
-            total = float(table[0, n]) * parts[0]
-            for m in range(1, NI):
-                total = total + float(table[m, n]) * parts[m]
-            y_w[pl.ds((n * NV + v) * 8, 8), :] = total
-    def out_rows(i, c):
-        even = y_w[pl.ds(i * 8, 4, stride=2), :]
-        odd = y_w[pl.ds(i * 8 + 1, 4, stride=2), :]
-        out_ref[i] = jnp.where(lane4 < 64, pltpu.roll(even, 96, 1), pltpu.roll(odd, 32, 1))
-        return c
-
-    lax.fori_loop(0, NF, out_rows, 0, unroll=5)
-
     @pl.when(r == ROWS - 1)
     def _():
-        index_copies[2].wait_recv()
+        index_copies[0].wait_recv()
 
     @pl.when(r == 0)
     def _():
-        index_copies[0].wait_recv()
-
-    index_copies[1].wait_recv()
+        index_copies[1].wait_recv()
+
+    index_copies[2].wait_recv()
+    index_copies[3].wait_recv()
     for c in index_copies:
         c.wait_send()
     most = jnp.zeros((NS, NS), jnp.float32)
@@ -477,7 +496,7 @@
     f32, i32, bf16 = jnp.float32, jnp.int32, jnp.bfloat16
     return pl.pallas_call(
         kernel,
-        out_shape=(jax.ShapeDtypeStruct((NF, 4, 128), f32), jax.ShapeDtypeStruct((1, 1), i32)),
+        out_shape=(jax.ShapeDtypeStruct((512, 128), f32), jax.ShapeDtypeStruct((1, 1), i32)),
         in_specs=[any_space] * 8,
         out_specs=(vmem, pl.BlockSpec(memory_space=pltpu.SMEM)),
         scratch_shapes=[
@@ -492,9 +511,6 @@
             pltpu.VMEM((1024, 128), f32),
             pltpu.VMEM((2, 128, 128), f32),
             pltpu.VMEM((NOFF, 8, 128), i32),
-            pltpu.VMEM((512, 128), f32),
-            pltpu.VMEM((512, 128), f32),
-            pltpu.VMEM((384, 128), f32),
             pltpu.VMEM((HALO_ROWS, 128), f32),
             pltpu.VMEM((HALO_ROWS, 128), f32),
             pltpu.VMEM((HALO_ROWS, 128), f32),
@@ -624,8 +640,8 @@
 
 
 def on_device(*args):
-    result, flag = fast(*args)
-    return lax.cond(flag[0, 0] > 0, lambda: general(*args), lambda: jnp.where(flag[0, 0] > 1, 0.0, result).reshape(1, NI, NV, OWN))
+    modes, flag = fast(*args)
+    return lax.cond(flag[0, 0] > 0, lambda: general(*args), lambda: finish(modes))
 
 
 def solution(mesh):

time: 46.7 us -> 41.9 us (0.90)
  Pallas kernels: 44.4 us -> 40.2 us
  loops' own time: 0.86 us -> 0.24 us
    pallas_call x1 -> x2, Pallas kernels: 44.4 us -> 40.2 us  [the longest x1 39.7 us: fast(): pl.pallas_call(kernel, out_shape=(jax.ShapeDtypeStruct((512, 128), f32),...]
    another operation x1, loops' own time: 0.86 us -> 0.24 us  [on_device(): lax.cond(flag[0, 0] > 0, lambda: general(*args), lambda: finish(modes))]
where the time goes in v3:
time: 41.9 us; the launch traced here: 41.8 us
  Pallas kernels  40.2 us (96%)
  between operations  0.7 us (2%)
  local copies, waits for them, and re-layouts  0.63 us (2%)
    pallas_call x1, Pallas kernels, fast(): pl.pallas_call(kernel, out_shape=(jax.ShapeDtypeStruct((512, 128), f32),...  39.7 us

profile of v3, /device:TPU:25, one launch (start us, length us, event | category | flops | bytes accessed | tf_op | source)
XLA Modules:
  0.0 41.8 jit_solution(15371048870864298029)
XLA Ops:
  0.0 39.7 %shard_map.84 = (f32[512,128]{1,0:T(8,128)S(1)}, s32[1,1]{1,0:T(1,128)}) custom-call(f32[45,4,128]{2,1,0:T(4,128)} %bitcast.195, f32[30,4,128]{2,1,0:T(4,128)} %bitcast.201, s32[6,4,128]{2,1,0:T(4,128)} %bitcast.208, f32[25,4,128]{2,1,0:T(4,128)} %bitcast.202, f32[100,4,512]{2,1,0:T(4,128)} %bitcast.192, s32[1,1024]{1,0:T(1,128)} %don_h.1, s32[1,1024]{1,0:T(1,128)} %rec_h.1, ...), custom_call_target="tpu_custom_call" | custom-call | tf_op jit(solution)/shard_map/pallas_call | solution.py:497
  40.4 0.8 %conditional.1 = (f32[1,9,5,512]{3,0,2,1:T(1,128)S(1)}) conditional(s32[]{:T(128)} %bitcast.50, f32[512,128]{1,0:T(8,128)S(1)} %get-tuple-element.150, (f32[1,9,5,512]{3,0,2,1:T(1,128)}, s32[1,1024]{1,0:T(1,128)}, f32[1,5,5,512]{3,0,2,1:T(1,128)}, f32[1,4,10,10,512]{4,1,3,2,0:T(4,128)}, s32[1,1024]{1,0:T(1,128)}, /*index=5*/f32[1,5,1024]{2,0,1:T(1,128)}, ...), branch_computations={%region_0.0_spmd, %region_1.12_spmd} | conditional | flops 11981840 | bytes 23738944 | solution.py:644
  40.4 0.5 %branch_0_fun.1 = f32[45,4,128]{2,1,0:T(4,128)S(1)} custom-call(f32[512,128]{1,0:T(8,128)S(1)} %x_w), custom_call_target="tpu_custom_call" | custom-call | flops 829440 | bytes 500000 | tf_op jit(solution)/shard_map/cond/branch_0_fun/pallas_call | solution.py:73
  41.2 0.0 copy-start.16
  41.2 0.6 %copy-done.16 = f32[1,9,5,512]{3,0,2,1:T(1,128)} copy-done((f32[1,9,5,512]{3,0,2,1:T(1,128)}, f32[1,9,5,512]{3,0,2,1:T(1,128)S(1)}, u32[]{:S(2)}) %copy-start.16) | copy-done | bytes 92184
Async XLA Ops:
  41.2 0.6 %copy-start.16 = (f32[1,9,5,512]{3,0,2,1:T(1,128)}, f32[1,9,5,512]{3,0,2,1:T(1,128)S(1)}, u32[]{:S(2)}) copy-start(f32[1,9,5,512]{3,0,2,1:T(1,128)S(1)} %get-tuple-element.619) | copy-start | bytes 276484

commit v4 on v3

--- a/solution.py
+++ b/solution.py
@@ -19,9 +19,10 @@
 ROWS = 4
 NS = 64
 GROUP = 8
+FAR = (4, 3, 5, 2, 6, 1, 7, 0)
 OWN = 512
 EDGE = 32
-CAP = 8
+CAP = 6
 MESH = pl.DeviceIdType.MESH
 
 HALO_ROWS = 136
@@ -100,21 +101,21 @@
     @pl.when(r < ROWS - 1)
     def _():
         for j in range(GROUP):
-            greet(r + 1, j * GROUP + p)
+            greet(r + 1, z * GROUP + j)
 
     @pl.when(r > 0)
     def _():
         for j in range(GROUP):
-            greet(r - 1, j * GROUP + p)
-
-    for j in range(1, GROUP):
-        greet(r, z * GROUP + lax.rem(p + j, GROUP))
-
-    @pl.when((p == 0) & (s > 0))
+            greet(r - 1, z * GROUP + j)
+
+    for d in FAR[:-1]:
+        greet(r, lax.rem(z + d, GROUP) * GROUP + p)
+
+    @pl.when(s > 0)
     def _():
         greet(r, s - 1)
 
-    @pl.when((p == GROUP - 1) & (s < NS - 1))
+    @pl.when(s < NS - 1)
     def _():
         greet(r, s + 1)
 
@@ -163,29 +164,18 @@
 
     loads[0].wait()
 
-    def wave_units(first, count, row):
-        firsts, lasts = [], []
-        for e in range(count):
-            tiles = [
-                jnp.concatenate([bw_v[2 * (first + e) + i, :, pl.ds(128 * m, 128)] for i in range(2)], axis=0)
-                for m in range(4)
-            ]
-            to_windows(tiles, wave_w, (first + e) * 64)
-            firsts.append(tiles[0])
-            lasts.append(tiles[3])
-        pack(firsts, lasts, row)
-
-    def wave_rows(p, c):
-        wave_units(4 * p, 4, 8 * p)
+    def wave_tile(u, m):
+        return jnp.concatenate([bw_v[2 * u + i, :, pl.ds(128 * m, 128)] for i in range(2)], axis=0)
+
+    def wave_pack(p, c):
+        pack([wave_tile(4 * p + e, 0) for e in range(4)], [wave_tile(4 * p + e, 3) for e in range(4)], 8 * p)
         return c
 
-    lax.fori_loop(0, 12, wave_rows, 0, unroll=3)
-    wave_units(48, 2, 96)
+    lax.fori_loop(0, 12, wave_pack, 0, unroll=4)
+    pack([wave_tile(48 + e, 0) for e in range(2)], [wave_tile(48 + e, 3) for e in range(2)], 96)
 
     for c in loads[1:5]:
         c.wait()
-    lane4 = lane8[:4]
-    row4 = lax.broadcasted_iota(jnp.int32, (4, 128), 0)
     table = spectral_numbers()
     for v in range(NV):
         parts = [rhs_v[n * NV + v] for n in range(NI)]
@@ -195,19 +185,13 @@
                 total = total + float(table[m, n]) * parts[n]
             rhs_v[m * NV + v] = total
 
-    for ref, skip, first, count in (
-            (bm_v, 0, 0, 25), (cpl_v, 0, 25, 30), (off_v, 0, 55, 6), (rhs_v, 0, 64, 25), (rhs_v, 25, 96, 20)):
-        def base_rows(i, c, ref=ref, skip=skip, first=first):
+    base_parts = (
+        (bm_v, 0, 0, 25), (cpl_v, 0, 25, 30), (off_v, 0, 55, 6), (rhs_v, 0, 64, 25), (rhs_v, 25, 96, 20))
+    for ref, skip, first, count in base_parts:
+        for i in range(count):
             tile = ref[skip + i].astype(jnp.float32)
-            up = pltpu.roll(tile, 32, 1)
-            down = pltpu.roll(tile, 96, 1)
-            at = (first + i) * 8
-            base_w[pl.ds(at, 4, stride=2), :] = jnp.where(lane4 < 32, pltpu.roll(up, 1, 0), up)
-            base_w[pl.ds(at + 1, 4, stride=2), :] = jnp.where(lane4 < 96, down, pltpu.roll(down, 3, 0))
             edge_s[0, pl.ds(first + i, 1), :] = tile[0:1]
             edge_s[1, pl.ds(first + i, 1), :] = tile[3:4]
-            return c
-        lax.fori_loop(0, count, base_rows, 0, unroll=5 if count % 5 == 0 else 6)
     for first, count in ((61, 3), (89, 7), (116, 12)):
         edge_s[:, pl.ds(first, count), :] = jnp.zeros((2, count, 128), jnp.float32)
         base_w[pl.ds(first * 8, count * 8), :] = jnp.zeros((count * 8, 128), jnp.float32)
@@ -233,9 +217,15 @@
         return jnp.where(condition, 1, 0)
 
     here = GROUP * (one_if(r > 0) + one_if(r < ROWS - 1)) + GROUP - 1
-    here = here + one_if((p == 0) & (s > 0)) + one_if((p == GROUP - 1) & (s < NS - 1))
+    here = here + one_if(s > 0) + one_if(s < NS - 1)
     here = here + 1 + one_if(r == 0) + one_if(r == ROWS - 1)
     pl.semaphore_wait(bar, here)
+
+    @pl.when(r > 0)
+    def _():
+        for j in range(GROUP):
+            at = (r - 1, z * GROUP + j)
+            pl.semaphore_signal(ready, inc=1, device_id=at, device_id_type=MESH)
 
     def index_copy(d, part, sem):
         at = idx_v.at[r] if part is None else idx_v.at[r, part]
@@ -263,10 +253,22 @@
     for c in index_copies[1:]:
         c.start()
 
-    @pl.when(r > 0)
-    def _():
-        for j in range(GROUP):
-            pl.semaphore_signal(ready, inc=1, device_id=(r - 1, j * GROUP + p), device_id_type=MESH)
+    def wave_windows(u, c):
+        to_windows([wave_tile(u, m) for m in range(4)], wave_w, u * 64)
+        return c
+
+    lax.fori_loop(0, 50, wave_windows, 0, unroll=10)
+    lane4 = lane8[:4]
+    for ref, skip, first, count in base_parts:
+        def base_rows(i, c, ref=ref, skip=skip, first=first):
+            tile = ref[skip + i].astype(jnp.float32)
+            up = pltpu.roll(tile, 32, 1)
+            down = pltpu.roll(tile, 96, 1)
+            at = (first + i) * 8
+            base_w[pl.ds(at, 4, stride=2), :] = jnp.where(lane4 < 32, pltpu.roll(up, 1, 0), up)
+            base_w[pl.ds(at + 1, 4, stride=2), :] = jnp.where(lane4 < 96, down, pltpu.roll(down, 3, 0))
+            return c
+        lax.fori_loop(0, count, base_rows, 0, unroll=5 if count % 5 == 0 else 6)
 
     dev64 = lax.broadcasted_iota(jnp.int32, (NS, 1), 0)
     tri = (lax.broadcasted_iota(jnp.int32, (128, 128), 0) <= lax.broadcasted_iota(jnp.int32, (128, 128), 1))
@@ -320,7 +322,7 @@
         for k in range(2):
             rows = jnp.zeros((NS, 128), jnp.float32)
             for v in range(NV):
-                for g in range(4):
+                for g in range(CAP // 2):
                     mine = (field % NV == v) & (field < 25) & (lane // 32 == g)
                     rows = rows + jnp.where(mine, pick(2 * g + k, gain_v[v]), 0.0)
             gpk_s[pl.ds(k * NS, NS), :] = rows
@@ -366,7 +368,7 @@
             device_id=(r - 1, s), device_id_type=MESH).wait_recv()
         rows = jnp.concatenate([got_s[h, :, k, :] for k in range(2)], axis=0) * gpk_s[...]
         turned = rows.T
-        both = jnp.concatenate([turned[32 * g:32 * g + 32] for g in range(4)], axis=1)
+        both = jnp.concatenate([turned[32 * g:32 * g + 32] for g in range(CAP // 2)], axis=1)
         high = both.astype(jnp.bfloat16)
         low = (both - high.astype(jnp.float32)).astype(jnp.bfloat16)
         added = jnp.dot(jnp.concatenate([high, low], axis=0), wr_s[...], preferred_element_type=jnp.float32)
@@ -402,14 +404,15 @@
             x_w[pl.ds(row + f * 8, 8), :] = x[f]
 
     def harmonic(k, c):
-        row = jnp.where(k < 2, 40 + 80 * k, 256 + 80 * (k - 2))
+        row = 40 + 80 * k if k < 2 else 256 + 80 * (k - 2)
         relax(row, 10, lambda f, g: wave_w[pl.ds((f * 10 + g) * 32 + k * 8, 8), :])
         return c
 
     def relax_half(h):
         if h == 0:
             relax(0, NV, lambda f, g: base_w[pl.ds((f * NV + g) * 8, 8), :])
-        lax.fori_loop(2 * h, 2 * h + 2, harmonic, 0, unroll=2)
+        for k in (2 * h, 2 * h + 1):
+            harmonic(k, 0)
 
     def donate(h):
         for a in range(2):
@@ -425,14 +428,14 @@
         values = values[:, :128] + values[:, 128:]
         for k in range(2):
             rows = values[k * NS:(k + 1) * NS]
-            for g in range(1, 4):
+            for g in range(1, CAP // 2):
                 at = (2 * g + k) * NS
                 rows = rows + pltpu.roll(values[at:at + NS], 32 * g, 1)
             msg_s[h, :, k, :] = rows
         if h == 0:
             pl.semaphore_wait(ready, GROUP)
 
-        for d in (4, 3, 5, 2, 6, 1, 7, 0):
+        for d in FAR:
             plane = lax.rem(z + d, GROUP) * GROUP
             for j in range(GROUP):
                 t = plane + j

time: 41.9 us -> 40.3 us (0.962)
  Pallas kernels: 40.2 us -> 38.6 us
    pallas_call x1, Pallas kernels: 39.7 us -> 38.1 us  [fast(): pl.pallas_call(kernel, out_shape=(jax.ShapeDtypeStruct((512, 128), f32),...]
where the time goes in v4:
time: 40.3 us; the launch traced here: 40.2 us
  Pallas kernels  38.6 us (96%)
  between operations  0.7 us (2%)
  local copies, waits for them, and re-layouts  0.63 us (2%)
    pallas_call x1, Pallas kernels, fast(): pl.pallas_call(kernel, out_shape=(jax.ShapeDtypeStruct((512, 128), f32),...  38.1 us

profile of v4, /device:TPU:25, one launch (start us, length us, event | category | flops | bytes accessed | tf_op | source)
XLA Modules:
  0.0 40.2 jit_solution(11181092942418758619)
XLA Ops:
  0.0 38.1 %shard_map.84 = (f32[512,128]{1,0:T(8,128)S(1)}, s32[1,1]{1,0:T(1,128)}) custom-call(f32[45,4,128]{2,1,0:T(4,128)} %bitcast.195, f32[30,4,128]{2,1,0:T(4,128)} %bitcast.201, s32[6,4,128]{2,1,0:T(4,128)} %bitcast.208, f32[25,4,128]{2,1,0:T(4,128)} %bitcast.202, f32[100,4,512]{2,1,0:T(4,128)} %bitcast.192, s32[1,1024]{1,0:T(1,128)} %don_h.1, s32[1,1024]{1,0:T(1,128)} %rec_h.1, ...), custom_call_target="tpu_custom_call" | custom-call | tf_op jit(solution)/shard_map/pallas_call | solution.py:500
  38.8 0.8 %conditional.1 = (f32[1,9,5,512]{3,0,2,1:T(1,128)S(1)}) conditional(s32[]{:T(128)} %bitcast.50, f32[512,128]{1,0:T(8,128)S(1)} %get-tuple-element.150, (f32[1,9,5,512]{3,0,2,1:T(1,128)}, s32[1,1024]{1,0:T(1,128)}, f32[1,5,5,512]{3,0,2,1:T(1,128)}, f32[1,4,10,10,512]{4,1,3,2,0:T(4,128)}, s32[1,1024]{1,0:T(1,128)}, /*index=5*/f32[1,5,1024]{2,0,1:T(1,128)}, ...), branch_computations={%region_0.0_spmd, %region_1.12_spmd} | conditional | flops 11981840 | bytes 23738944 | solution.py:647
  38.8 0.5 %branch_0_fun.1 = f32[45,4,128]{2,1,0:T(4,128)S(1)} custom-call(f32[512,128]{1,0:T(8,128)S(1)} %x_w), custom_call_target="tpu_custom_call" | custom-call | flops 829440 | bytes 500000 | tf_op jit(solution)/shard_map/cond/branch_0_fun/pallas_call | solution.py:74
  39.5 0.0 copy-start.16
  39.5 0.6 %copy-done.16 = f32[1,9,5,512]{3,0,2,1:T(1,128)} copy-done((f32[1,9,5,512]{3,0,2,1:T(1,128)}, f32[1,9,5,512]{3,0,2,1:T(1,128)S(1)}, u32[]{:S(2)}) %copy-start.16) | copy-done | bytes 92184
Async XLA Ops:
  39.5 0.6 %copy-start.16 = (f32[1,9,5,512]{3,0,2,1:T(1,128)}, f32[1,9,5,512]{3,0,2,1:T(1,128)S(1)}, u32[]{:S(2)}) copy-start(f32[1,9,5,512]{3,0,2,1:T(1,128)S(1)} %get-tuple-element.619) | copy-start | bytes 276484

commit v5 on v4

--- a/solution.py
+++ b/solution.py
@@ -74,7 +74,7 @@
     return pl.pallas_call(
         finish_kernel,
         out_shape=jax.ShapeDtypeStruct((NF, 4, 128), jnp.float32),
-        scratch_shapes=[pltpu.VMEM((NF * 8, 128), jnp.float32)],
+        scratch_shapes=[pltpu.VMEM((NF * 8 + 8, 128), jnp.float32)],
         cost_estimate=pl.CostEstimate(flops=2 * NI * NF * 1024, bytes_accessed=500000, transcendentals=0),
     )(modes).reshape(1, NI, NV, OWN)
 
@@ -201,9 +201,8 @@
             [edge_s[1, pl.ds(32 * e + 8 * q, 8), :] for e in range(4)], AT_BASE + 8 * q)
     for c in loads[5:]:
         c.wait()
-    xr_s[...] = jnp.zeros(xr_s.shape, jnp.bfloat16)
     x_w[pl.ds(200, 56), :] = jnp.zeros((56, 128), jnp.float32)
-    x_w[pl.ds(416, 96), :] = jnp.zeros((96, 128), jnp.float32)
+    x_w[pl.ds(416, 104), :] = jnp.zeros((104, 128), jnp.float32)
 
     @pl.when(s == 0)
     def _():
@@ -422,16 +421,15 @@
                 high = tile.astype(jnp.bfloat16)
                 low = (tile - high.astype(jnp.float32)).astype(jnp.bfloat16)
                 xr_s[pl.ds(16 * a, 16), pl.ds(128 * m, 128)] = high
-                xr_s[pl.ds(128 + 16 * a, 16), pl.ds(128 * m, 128)] = low
+                xr_s[pl.ds(32 + 16 * a, 16), pl.ds(128 * m, 128)] = low
         values = lax.dot_general(
-            sel_s[...], xr_s[...], (((1,), (1,)), ((), ())), preferred_element_type=jnp.float32)
-        values = values[:, :128] + values[:, 128:]
+            xr_s[...], sel_s[...], (((1,), (1,)), ((), ())), preferred_element_type=jnp.float32)
+        values = values[:32] + values[32:]
+        groups = [values[:, 128 * g:128 * g + 128] for g in range(CAP // 2)]
+        groups += [jnp.zeros((32, 128), jnp.float32)] * (4 - CAP // 2)
+        rows = jnp.concatenate(groups, axis=0).T
         for k in range(2):
-            rows = values[k * NS:(k + 1) * NS]
-            for g in range(1, CAP // 2):
-                at = (2 * g + k) * NS
-                rows = rows + pltpu.roll(values[at:at + NS], 32 * g, 1)
-            msg_s[h, :, k, :] = rows
+            msg_s[h, :, k, :] = rows[k * NS:(k + 1) * NS]
         if h == 0:
             pl.semaphore_wait(ready, GROUP)
 
@@ -443,6 +441,29 @@
                     msg_s.at[h, t], got_s.at[h, s], msg_send.at[h], msg_recv.at[h],
                     device_id=(r + 1, t), device_id_type=MESH).start()
 
+    def check():
+        @pl.when(r == ROWS - 1)
+        def _():
+            index_copies[0].wait_recv()
+
+        @pl.when(r == 0)
+        def _():
+            index_copies[1].wait_recv()
+
+        index_copies[2].wait_recv()
+        index_copies[3].wait_recv()
+        most = jnp.zeros((NS, NS), jnp.float32)
+        for row in range(ROWS - 1):
+            gives = in_block(idx_v[row, 0], dev64).astype(jnp.float32).astype(jnp.bfloat16)
+            takes = in_windows(idx_v[row + 1, 1], dev64).astype(jnp.float32).astype(jnp.bfloat16)
+            count = lax.dot_general(gives, takes, (((1,), (1,)), ((), ())), preferred_element_type=jnp.float32)
+            most = jnp.maximum(most, count)
+        flag_ref[0, 0] = jnp.where(jnp.max(most) > CAP + 0.5, 1, 0)
+
+    @pl.when(r > 0)
+    def _():
+        check()
+
     for h in range(2):
         @pl.when(r > 0)
         def _():
@@ -454,25 +475,12 @@
         def _():
             donate(h)
 
-    @pl.when(r == ROWS - 1)
-    def _():
-        index_copies[0].wait_recv()
-
     @pl.when(r == 0)
     def _():
-        index_copies[1].wait_recv()
-
-    index_copies[2].wait_recv()
-    index_copies[3].wait_recv()
+        check()
+
     for c in index_copies:
         c.wait_send()
-    most = jnp.zeros((NS, NS), jnp.float32)
-    for row in range(ROWS - 1):
-        gives = in_block(idx_v[row, 0], dev64).astype(jnp.float32).astype(jnp.bfloat16)
-        takes = in_windows(idx_v[row + 1, 1], dev64).astype(jnp.float32).astype(jnp.bfloat16)
-        count = lax.dot_general(gives, takes, (((1,), (1,)), ((), ())), preferred_element_type=jnp.float32)
-        most = jnp.maximum(most, count)
-    flag_ref[0, 0] = jnp.where(jnp.max(most) > CAP + 0.5, 1, 0)
 
     @pl.when(s < NS - 1)
     def _():
@@ -499,7 +507,7 @@
     f32, i32, bf16 = jnp.float32, jnp.int32, jnp.bfloat16
     return pl.pallas_call(
         kernel,
-        out_shape=(jax.ShapeDtypeStruct((512, 128), f32), jax.ShapeDtypeStruct((1, 1), i32)),
+        out_shape=(jax.ShapeDtypeStruct((520, 128), f32), jax.ShapeDtypeStruct((1, 1), i32)),
         in_specs=[any_space] * 8,
         out_specs=(vmem, pl.BlockSpec(memory_space=pltpu.SMEM)),
         scratch_shapes=[
@@ -510,7 +518,7 @@
             pltpu.VMEM((100, 4, OWN), f32),
             pltpu.VMEM((NV, 1, NIF), f32),
             pltpu.VMEM((ROWS, 2, 1, NIF), i32),
-            pltpu.VMEM((3200, 128), f32),
+            pltpu.VMEM((3208, 128), f32),
             pltpu.VMEM((1024, 128), f32),
             pltpu.VMEM((2, 128, 128), f32),
             pltpu.VMEM((NOFF, 8, 128), i32),
@@ -520,7 +528,7 @@
             pltpu.VMEM((HALO_ROWS, 128), f32),
             pltpu.VMEM((NS, NIF), f32),
             pltpu.VMEM((CAP * NS, OWN), bf16),
-            pltpu.VMEM((256, OWN), bf16),
+            pltpu.VMEM((64, OWN), bf16),
             pltpu.VMEM((CAP * NS, 1024), bf16),
             pltpu.VMEM((2 * NS, 128), f32),
             pltpu.VMEM((2, NS, 2, 128), f32),

time: 40.3 us -> 39.6 us (0.983)
  Pallas kernels: 38.6 us -> 37.9 us
    pallas_call x1, Pallas kernels: 38.1 us -> 37.4 us  [fast(): pl.pallas_call(kernel, out_shape=(jax.ShapeDtypeStruct((520, 128), f32),...]
where the time goes in v5:
time: 39.6 us; the launch traced here: 39.5 us
  Pallas kernels  37.9 us (96%)
  between operations  0.7 us (2%)
  local copies, waits for them, and re-layouts  0.63 us (2%)
    pallas_call x1, Pallas kernels, fast(): pl.pallas_call(kernel, out_shape=(jax.ShapeDtypeStruct((520, 128), f32),...  37.4 us

profile of v5, /device:TPU:25, one launch (start us, length us, event | category | flops | bytes accessed | tf_op | source)
XLA Modules:
  0.0 39.5 jit_solution(14746743077529317036)
XLA Ops:
  0.0 37.4 %shard_map.84 = (f32[520,128]{1,0:T(8,128)S(1)}, s32[1,1]{1,0:T(1,128)}) custom-call(f32[45,4,128]{2,1,0:T(4,128)} %bitcast.195, f32[30,4,128]{2,1,0:T(4,128)} %bitcast.201, s32[6,4,128]{2,1,0:T(4,128)} %bitcast.208, f32[25,4,128]{2,1,0:T(4,128)} %bitcast.202, f32[100,4,512]{2,1,0:T(4,128)} %bitcast.192, s32[1,1024]{1,0:T(1,128)} %don_h.1, s32[1,1024]{1,0:T(1,128)} %rec_h.1, ...), custom_call_target="tpu_custom_call" | custom-call | tf_op jit(solution)/shard_map/pallas_call | solution.py:508
  38.0 0.8 %conditional.1 = (f32[1,9,5,512]{3,0,2,1:T(1,128)S(1)}) conditional(s32[]{:T(128)} %bitcast.50, f32[520,128]{1,0:T(8,128)S(1)} %get-tuple-element.150, (f32[1,9,5,512]{3,0,2,1:T(1,128)}, s32[1,1024]{1,0:T(1,128)}, f32[1,5,5,512]{3,0,2,1:T(1,128)}, f32[1,4,10,10,512]{4,1,3,2,0:T(4,128)}, s32[1,1024]{1,0:T(1,128)}, /*index=5*/f32[1,5,1024]{2,0,1:T(1,128)}, ...), branch_computations={%region_0.0_spmd, %region_1.12_spmd} | conditional | flops 11981840 | bytes 23738944 | solution.py:655
  38.1 0.5 %branch_0_fun.1 = f32[45,4,128]{2,1,0:T(4,128)S(1)} custom-call(f32[520,128]{1,0:T(8,128)S(1)} %x_w), custom_call_target="tpu_custom_call" | custom-call | flops 829440 | bytes 500000 | tf_op jit(solution)/shard_map/cond/branch_0_fun/pallas_call | solution.py:74
  38.8 0.0 copy-start.16
  38.8 0.6 %copy-done.16 = f32[1,9,5,512]{3,0,2,1:T(1,128)} copy-done((f32[1,9,5,512]{3,0,2,1:T(1,128)}, f32[1,9,5,512]{3,0,2,1:T(1,128)S(1)}, u32[]{:S(2)}) %copy-start.16) | copy-done | bytes 92184
Async XLA Ops:
  38.8 0.6 %copy-start.16 = (f32[1,9,5,512]{3,0,2,1:T(1,128)}, f32[1,9,5,512]{3,0,2,1:T(1,128)S(1)}, u32[]{:S(2)}) copy-start(f32[1,9,5,512]{3,0,2,1:T(1,128)S(1)} %get-tuple-element.619) | copy-start | bytes 276484
